TPU v7x, 256 devices: a whole 4x4x8 slice. The times are simulated.
256 devices in a mesh: sec: 2 (over x_lo), gx: 64 (over y, z, core), gy: 2 (over x_hi).
Axes of the slice: x: 4 (x_hi: 2, x_lo: 2; x = x_hi * 2 + x_lo), y: 4, z: 8, core: 2. Of those that a mesh axis runs over, the one named last changes fastest.
Arguments:
- initial_unknowns: float32 [2, 2, 256, 128, 256], P('sec', None, 'gx', 'gy'), may hold values from -3.5 to 3.5, as said below
- section_coeffs: float32 [2, 4, 256, 128, 256], P('sec', None, 'gx', 'gy'), may hold values from 0.005 to 20, as said below
- rock_type: int32 [256, 128, 256], P('gx', 'gy'), may hold values from 0 to 7
- rock_table: float32 [8, 3], replicated, may hold values from 0.3 to 1
- opening_grid_location: int32 [32768], P(('gx', 'gy')), may hold values from 0 to 65535
- perf_well: int32 [32768], P(('gx', 'gy')), may hold values from -1 to 8191, as said below
- well_index: float32 [32768], P(('gx', 'gy')), may hold values from 0.5 to 5
- perf_pressure: float32 [32768], P(('gx', 'gy')), may hold values from -5 to 5
- well_owner: int32 [8192], replicated, may hold values from 0 to 127, as said below
- well_slot: int32 [8192], replicated, may hold values from 0 to 127, as said below
Outputs:
- closing_unknowns: float32 [2, 2, 256, 128, 256], P('sec', None, 'gx', 'gy')
- well_rates: float32 [2, 2, 16384], P('sec', None, ('gx', 'gy'))
Inputs may be any that keep to these rules, and one draw needn't show every extreme that they name: `initial_unknowns`: section 0 holds pressure, then temperature within 0.5 to 1.5; section 1 holds water saturation within 0.1 to 0.5, then gas saturation within 0.05 to 0.3. `section_coeffs`: all positive: permeabilities within 0.005 to 20, accumulation coefficients within 0.3 to 3, conductivities within 0.2 to 2, pore volumes over the time step within 2 to 8, viscosities of water within 0.3 to 1, of oil within 1 to 10, of gas within 0.05 to 0.3. `perf_well`: -1 marks an empty slot; in each block of 256 slots the live ones come first and at least 64 are live; some block has all of them live. `well_owner`: owner blocks are numbered along gx+gy with gx slowest; no owner holds more than 128 wells and some owner holds exactly 128. `well_slot`: no two wells share both owner and slot.
All inputs are finite; a program needn't handle non-finite values.
Results may differ from a plain program's by a relative error of at most 0.00015.
Values sent between devices are 32-bit elements; how exact they have to be, the bound alone decides.
A program may use at most 64 MiB of HBM per device.

v0:
```python
import jax
import jax.numpy as jnp
from jax import lax
from jax.sharding import PartitionSpec as P

WSLOT = 128
SWEEPS = 2
NROCK = 8


THERMAL_LINKED = 1.5
EXACT = lax.Precision.HIGHEST


def extended(value, sides, width):
    for axis, dim in sides:
        size, length = (lax.axis_size(axis), value.shape[dim])
        up = [(i, (i + 1) % size) for i in range(size - 1)]
        down = [(j, i) for i, j in up]
        last = lax.slice_in_dim(value, length - width, length, axis=dim)
        leading = lax.slice_in_dim(value, 0, width, axis=dim)
        before = lax.ppermute(last, axis, up)
        after = lax.ppermute(leading, axis, down)
        value = jnp.concatenate([before, value, after], axis=dim)
    return value


def shifted(value, axis, by):
    size = lax.axis_size(axis)
    pairs = [(i, i + by) for i in range(size) if 0 <= i + by < size]
    return lax.ppermute(value, axis, pairs)


def guarded_quotient(numerator, denominator):
    return numerator / jnp.where(denominator > 0, denominator, 1.0)


def harmonic(lower_value, upper_value):
    return guarded_quotient(2.0 * lower_value * upper_value, lower_value + upper_value)


def relaxation_sweep_pass(
    current, lateral_darcy_flux, base, storage_summands, vertical, well_diag, well_rhs
):
    east_face = harmonic(lateral_darcy_flux[1:, 1:-1], lateral_darcy_flux[:-1, 1:-1])
    north_face = harmonic(lateral_darcy_flux[1:-1, 1:], lateral_darcy_flux[1:-1, :-1])
    upper_face = harmonic(vertical[:, :, 1:], vertical[:, :, :-1])
    flat_zero = jnp.zeros_like(upper_face[:, :, :1])
    upward = jnp.concatenate([upper_face, flat_zero], axis=2)
    downward = jnp.concatenate([flat_zero, upper_face], axis=2)
    centre = current[1:-1, 1:-1]
    below_cell = jnp.concatenate([flat_zero, centre[:, :, :-1]], axis=2)
    above_cell = jnp.concatenate([centre[:, :, 1:], flat_zero], axis=2)
    neighbour_sum = (
        east_face[:-1] * current[:-2, 1:-1]
        + east_face[1:] * current[2:, 1:-1]
        + north_face[:, :-1] * current[1:-1, :-2]
        + north_face[:, 1:] * current[1:-1, 2:]
        + downward * below_cell
        + upward * above_cell
    )
    coupling = (
        east_face[:-1] + east_face[1:] + north_face[:, :-1] + north_face[:, 1:] + downward + upward
    )
    numerator = storage_summands * base + well_rhs + neighbour_sum
    denominator = storage_summands + well_diag + coupling
    return guarded_quotient(numerator, denominator)


def face_parts(pressure_rim, horizontal_rim, vertical):
    east_face = harmonic(horizontal_rim[1:, 1:-1], horizontal_rim[:-1, 1:-1])
    flow_x = east_face * (pressure_rim[:-1, 1:-1] - pressure_rim[1:, 1:-1])
    north_face = harmonic(horizontal_rim[1:-1, 1:], horizontal_rim[1:-1, :-1])
    flow_y = north_face * (pressure_rim[1:-1, :-1] - pressure_rim[1:-1, 1:])
    upper_face = harmonic(vertical[:, :, 1:], vertical[:, :, :-1])
    centre = pressure_rim[1:-1, 1:-1]
    flow_z = upper_face * (centre[:, :, :-1] - centre[:, :, 1:])
    upward = jnp.concatenate([flow_z, jnp.zeros_like(flow_z[:, :, :1])], axis=2)
    return (flow_x, flow_y, upward)


def split_faces(flow_x, flow_y, upward):
    return (flow_x[:-1], flow_x[1:], flow_y[:, :-1], flow_y[:, 1:], upward)


def upwind_net(share_rim, flows):
    west_flow, east_flow, south_flow, north_flow, upward = flows
    centre = share_rim[1:-1, 1:-1]
    flat_zero = jnp.zeros_like(centre[:, :, :1])
    below_cell = jnp.concatenate([flat_zero, centre[:, :, :-1]], axis=2)
    above_cell = jnp.concatenate([centre[:, :, 1:], flat_zero], axis=2)
    downward = jnp.concatenate([flat_zero, upward[:, :, :-1]], axis=2)
    in_west = (
        jnp.maximum(west_flow, 0.0) * share_rim[:-2, 1:-1] + jnp.minimum(west_flow, 0.0) * centre
    )
    out_east = (
        jnp.maximum(east_flow, 0.0) * centre + jnp.minimum(east_flow, 0.0) * share_rim[2:, 1:-1]
    )
    in_south = (
        jnp.maximum(south_flow, 0.0) * share_rim[1:-1, :-2] + jnp.minimum(south_flow, 0.0) * centre
    )
    out_north = (
        jnp.maximum(north_flow, 0.0) * centre + jnp.minimum(north_flow, 0.0) * share_rim[1:-1, 2:]
    )
    in_down = jnp.maximum(downward, 0.0) * below_cell + jnp.minimum(downward, 0.0) * centre
    out_up = jnp.maximum(upward, 0.0) * centre + jnp.minimum(upward, 0.0) * above_cell
    return in_west - out_east + in_south - out_north + in_down - out_up


def well_partial(first_value, second_value, owner_index, slot_index, owners):
    owner_hot = (owner_index[:, None] == jnp.arange(owners, dtype=jnp.int32)[None, :]).astype(
        jnp.float32
    )
    slot_hot = (slot_index[:, None] == jnp.arange(WSLOT, dtype=jnp.int32)[None, :]).astype(
        jnp.float32
    )
    weighted = jnp.stack(
        [owner_hot * first_value[:, None], owner_hot * second_value[:, None]], axis=1
    )
    blocks = jnp.einsum("pqo,ps->qos", weighted, slot_hot, precision=EXACT)
    return blocks.reshape(2, owners * WSLOT)


def per_device(
    initial_unknowns,
    section_coeffs,
    rock_type,
    rock_table,
    opening_grid_location,
    perf_well,
    well_index,
    perf_pressure,
    well_owner,
    well_slot,
):
    section = lax.axis_index("sec")
    unknowns_sequence = initial_unknowns[0]
    coeffs = section_coeffs[0]
    span_first, span_second, depth_cells = unknowns_sequence.shape[1:]
    mesh_extents = (span_first, span_second, depth_cells)
    number_nodes = span_first * span_second * depth_cells
    perf_count = opening_grid_location.shape[0]
    owners = lax.axis_size("gx") * lax.axis_size("gy")
    live_slot = perf_well >= 0
    well_id = jnp.maximum(perf_well, 0)
    owner_index = jnp.take(well_owner, well_id)
    slot_index = jnp.take(well_slot, well_id)
    x_count = (span_first + 1) * span_second * depth_cells
    y_count = span_first * (span_second + 1) * depth_cells

    def perf_rates(at_cell):
        return jnp.where(live_slot, well_index * (perf_pressure - at_cell), 0.0)

    fluid_head_before = unknowns_sequence[0]
    kelvin_level_before = unknowns_sequence[1]
    lateral_darcy_flux = coeffs[0]
    vertical = coeffs[1]
    storage_summands = coeffs[2]
    thermal_diffusion = coeffs[3]
    live_index = jnp.where(live_slot, well_index, 0.0)
    well_diag = (
        jnp.zeros((number_nodes,), jnp.float32)
        .at[opening_grid_location]
        .add(live_index)
        .reshape(mesh_extents)
    )
    well_rhs = (
        jnp.zeros((number_nodes,), jnp.float32)
        .at[opening_grid_location]
        .add(live_index * perf_pressure)
        .reshape(mesh_extents)
    )
    front_halo_layer = extended(
        jnp.stack([fluid_head_before, kelvin_level_before, lateral_darcy_flux, thermal_diffusion]),
        (("gx", 1), ("gy", 2)),
        1,
    )
    pressure_rim = front_halo_layer[0]
    thermal_halo_layer = front_halo_layer[1]
    for sweep_index in range(SWEEPS):
        if sweep_index > 0:
            rear_halo_layer = extended(
                jnp.stack([present_pressure_height, present_absolute_warmth]),
                (("gx", 1), ("gy", 2)),
                1,
            )
            pressure_rim = rear_halo_layer[0]
            thermal_halo_layer = rear_halo_layer[1]
        present_pressure_height = relaxation_sweep_pass(
            pressure_rim,
            front_halo_layer[2],
            fluid_head_before,
            storage_summands,
            vertical,
            well_diag,
            well_rhs,
        )
        present_absolute_warmth = relaxation_sweep_pass(
            thermal_halo_layer,
            front_halo_layer[3],
            kelvin_level_before,
            storage_summands,
            thermal_diffusion,
            0.0,
            0.0,
        )
    final_warmth_state = present_absolute_warmth
    horizontal_rim = front_halo_layer[2]
    pressure_rim = extended(present_pressure_height, (("gx", 0), ("gy", 1)), 1)
    at_cell = present_pressure_height.reshape(-1)[opening_grid_location]
    flow_x, flow_y, upward = face_parts(pressure_rim, horizontal_rim, vertical)
    face_plane_block = jnp.concatenate(
        [
            flow_x.reshape(-1),
            flow_y.reshape(-1),
            upward.reshape(-1),
            final_warmth_state.reshape(-1),
            at_cell,
        ]
    )
    opening_inflow_rate = perf_rates(at_cell)
    injected_heat_amount = (
        opening_inflow_rate * final_warmth_state.reshape(-1)[opening_grid_location]
    )
    partial_result = well_partial(
        opening_inflow_rate, injected_heat_amount, owner_index, slot_index, owners
    )
    pressure_new, face_plane_block, pressure_partial = (
        jnp.stack([present_pressure_height, final_warmth_state]),
        face_plane_block,
        partial_result,
    )
    incoming_neighbour_data = shifted(face_plane_block, "sec", 1)
    aqueous_saturation = unknowns_sequence[0]
    vapour_saturation = unknowns_sequence[1]
    pore_volume = coeffs[0]
    visc_water = coeffs[1]
    crude_dynamic_stickiness = coeffs[2]
    vapour_viscosity = coeffs[3]
    initial_displacement = 0
    flow_x = incoming_neighbour_data[initial_displacement : initial_displacement + x_count].reshape(
        span_first + 1, span_second, depth_cells
    )
    initial_displacement = initial_displacement + x_count
    flow_y = incoming_neighbour_data[initial_displacement : initial_displacement + y_count].reshape(
        span_first, span_second + 1, depth_cells
    )
    initial_displacement = initial_displacement + y_count
    upward = incoming_neighbour_data[
        initial_displacement : initial_displacement + number_nodes
    ].reshape(mesh_extents)
    initial_displacement = initial_displacement + number_nodes
    present_absolute_warmth = incoming_neighbour_data[
        initial_displacement : initial_displacement + number_nodes
    ].reshape(mesh_extents)
    initial_displacement = initial_displacement + number_nodes
    at_cell = incoming_neighbour_data[initial_displacement : initial_displacement + perf_count]
    rock_hot = (rock_type[None] == jnp.arange(NROCK, dtype=jnp.int32)[:, None, None, None]).astype(
        jnp.float32
    )
    far_endpoint = jnp.einsum("rabc,rk->kabc", rock_hot, rock_table, precision=EXACT)
    crude_saturation = 1.0 - aqueous_saturation - vapour_saturation
    water_mobility = far_endpoint[0] * aqueous_saturation * aqueous_saturation / visc_water
    crude_relative_transport = (
        far_endpoint[1]
        * crude_saturation
        * crude_saturation
        * jnp.exp(THERMAL_LINKED * (present_absolute_warmth - 1.0))
        / crude_dynamic_stickiness
    )
    gas_mobility = far_endpoint[2] * vapour_saturation * vapour_saturation / vapour_viscosity
    total_mobility = water_mobility + crude_relative_transport + gas_mobility
    water_share = guarded_quotient(water_mobility, total_mobility)
    gas_share = guarded_quotient(gas_mobility, total_mobility)
    share_rim = extended(jnp.stack([water_share, gas_share]), (("gx", 1), ("gy", 2)), 1)
    flows = split_faces(flow_x, flow_y, upward)
    opening_inflow_rate = perf_rates(at_cell)
    cell_rate = (
        jnp.zeros((number_nodes,), jnp.float32)
        .at[opening_grid_location]
        .add(opening_inflow_rate)
        .reshape(mesh_extents)
    )
    aqueous_saturation_new = (
        aqueous_saturation
        + (upwind_net(share_rim[0], flows) + cell_rate * water_share) / pore_volume
    )
    vapour_saturation_new = (
        vapour_saturation + (upwind_net(share_rim[1], flows) + cell_rate * gas_share) / pore_volume
    )
    partial_result = well_partial(
        opening_inflow_rate * water_share.reshape(-1)[opening_grid_location],
        opening_inflow_rate * gas_share.reshape(-1)[opening_grid_location],
        owner_index,
        slot_index,
        owners,
    )
    transport_new = jnp.stack([aqueous_saturation_new, vapour_saturation_new])
    transport_partial = partial_result
    closing_unknowns = jnp.where(section == 0, pressure_new, transport_new)[None]
    partial_result = jnp.where(section == 0, pressure_partial, transport_partial)
    summed = lax.psum_scatter(partial_result, ("gx", "gy"), scatter_dimension=1, tiled=True)
    return (closing_unknowns, summed[None])


def solution(mesh):
    in_specs = (
        P("sec", None, "gx", "gy", None),
        P("sec", None, "gx", "gy", None),
        P("gx", "gy", None),
        P(),
        P(("gx", "gy")),
        P(("gx", "gy")),
        P(("gx", "gy")),
        P(("gx", "gy")),
        P(),
        P(),
    )
    out_specs = (P("sec", None, "gx", "gy", None), P("sec", None, ("gx", "gy")))
    return jax.shard_map(
        per_device, mesh=mesh, in_specs=in_specs, out_specs=out_specs, check_vma=False
    )
```

profile of v0, /device:TPU:2, one launch (start us, length us, event | category | flops | bytes accessed | tf_op | source)
XLA Modules:
  0.0 838.5 jit_solution(5819004423028625550)
XLA Ops:
  7.2 1.9 fusion.119
  10.2 1.8 collective-permute-start
  14.2 2.9 collective-permute-done.1
  17.7 4.0 collective-permute-start.2
  23.1 2.0 scatter_custom_fusion
  25.9 2.0 scatter_custom_fusion.1
  32.1 6.1 collective-permute-start.4
  39.5 1.9 collective-permute-done.5
  41.5 5.8 collective-permute-start.6
  48.6 5.7 collective-permute-done.7
  57.1 5.2 collective-permute-start.8
  63.6 1.7 gather_fusion
  67.2 1.9 collective-permute-start.10
  71.2 5.0 collective-permute-done.11
  80.6 1.7 gather_fusion.5
  82.3 1.7 gather_fusion.4
  85.1 1.8 copy.35
  86.8 1.8 copy.33
  89.4 1.9 fusion.1
  92.0 2.3 gather_fusion.1
  94.3 13.3 %collective-permute-done.12 = f32[279808]{0:T(1024)} collective-permute-done((f32[279808]{0:T(1024)}, f32[279808]{0:T(1024)}, u32[]{:S(2)}, u32[]{:S(2)}) %collective-permute-start.12) | collective-permute-done | bytes 1119264 | tf_op jit(solution)/shard_map/ppermute | solution.py:31
  107.6 2.7 multiply_divide_fusion.1
  111.3 2.3 gather_fusion.3
  119.8 2.9 collective-permute-done.14
  123.3 1.9 collective-permute-start.15
  127.6 2.7 scatter_custom_fusion.2
  132.2 1.7 reshape.379
  134.9 1.7 max.34
  138.4 1.7 max.36
  140.1 1.7 min.33
  141.9 5.5 copy.24
  152.5 677.7 %reduce-scatter.4.cloned.1.call-done = f32[128,2]{1,0:T(8,128)} async-done(((f32[16384,2]{1,0:T(8,128)}), f32[128,2]{1,0:T(8,128)}) %reduce-scatter.4.cloned.1.call-update) | async-done | bytes 1040
  (165 shorter events, 48.3 us)
Async XLA Ops:
  7.2 73.4 %copy-start = (s32[8192]{0:T(1024)S(1)}, s32[8192]{0:T(1024)}, u32[]{:S(2)}) copy-start(s32[8192]{0:T(1024)} %param.21) | copy-start | bytes 98308
  7.2 823.0 %reduce-scatter.4.cloned.1.call-start = ((), (), s32[]{:S(2)}) async-start(), calls=%async_computation.1 | async-start | bytes 8454144
  9.2 4.1 copy-start.24
  9.2 4.1 copy-start.27
  9.2 4.1 copy-start.29
  10.2 12.9 %copy-start.34 = (s32[256]{0:T(256)S(1)}, s32[256]{0:T(256)}, u32[]{:S(2)}) copy-start(s32[256]{0:T(256)} %param.16) | copy-start | bytes 3076
  10.2 4.0 collective-permute-start
  12.0 5.1 collective-permute-start.1
  17.7 10.9 %collective-permute-start.2 = (f32[4,6,1,256]{3,2,1,0:T(1,128)}, f32[4,6,1,256]{3,2,1,0:T(1,128)S(1)}, u32[]{:S(2)}, u32[]{:S(2)}) collective-permute-start(f32[4,6,1,256]{3,2,1,0:T(1,128)} %get-tuple-element.19), channel_id=1, source_target_pairs={{0,1},{2,3},{4,5},{6,7},{8,9},{10,11},{12,13},{14,15},{16,17},{18,... | collective-permute-start | bytes 73736 | tf_op jit(solution)/shard_map/ppermute | solution.py:22
  21.8 7.2 collective-permute-start.3
  23.1 25.5 %copy-start.26 = (s32[256]{0:T(256)}, s32[256]{0:T(256)S(1)}, u32[]{:S(2)}) copy-start(s32[256]{0:T(256)S(1)} %compare_select_fusion.11) | copy-start | bytes 3076
  32.1 7.4 collective-permute-start.4
  38.2 3.2 collective-permute-start.5
  41.5 7.2 collective-permute-start.6
  47.2 7.1 collective-permute-start.7
  55.8 9.5 %collective-permute-start.9 = (f32[1,64,256]{2,1,0:T(8,128)}, f32[1,64,256]{2,1,0:T(8,128)}, u32[]{:S(2)}, u32[]{:S(2)}) collective-permute-start(f32[1,64,256]{2,1,0:T(8,128)} %get-tuple-element.69), channel_id=1, source_target_pairs={{2,0},{4,2},{6,4},{8,6},{10,8},{12,10},{14,12},{16,14},{18,16},{20... | collective-permute-start | bytes 196616 | tf_op jit(solution)/shard_map/ppermute | solution.py:23
  57.1 8.3 collective-permute-start.8
  67.2 4.0 collective-permute-start.10
  69.1 7.0 collective-permute-start.11
  76.2 6.1 copy-start.1
  76.3 7.8 copy-start.20
  79.1 28.5 %collective-permute-start.12 = (f32[279808]{0:T(1024)}, f32[279808]{0:T(1024)}, u32[]{:S(2)}, u32[]{:S(2)}) collective-permute-start(f32[279808]{0:T(1024)} %constant_dynamic-update-slice_fusion), channel_id=1, source_target_pairs={{0,128},{1,129},{2,130},{3,131},{4,132},{5,133},{6,134},{7,135},{8... | collective-permute-start | bytes 3357704 | tf_op jit(solution)/shard_map/ppermute | solution.py:31
  82.3 6.3 copy-start.21
  82.3 7.1 copy-start.33
  88.8 18.8 %copy-start.16 = (f32[32,2,8,128]{3,1,2,0:T(2,128)}, f32[32,2,8,128]{3,1,2,0:T(2,128)S(1)}, u32[]{:S(2)}) copy-start(f32[32,2,8,128]{3,1,2,0:T(2,128)S(1)} %copy.36) | copy-start | bytes 786436
  92.0 23.5 %copy-start.4 = (f32[1,4,64,256]{3,0,2,1:T(1,128)}, f32[1,4,64,256]{3,0,2,1:T(1,128)S(1)}, u32[]{:S(2)}) copy-start(f32[1,4,64,256]{3,0,2,1:T(1,128)S(1)} %get-tuple-element.28) | copy-start | bytes 786436
  111.3 4.1 copy-start.17
  115.8 14.5 %copy-start.18 = (f32[65536]{0:T(1024)S(1)}, f32[65536]{0:T(1024)}, u32[]{:S(2)}) copy-start(f32[65536]{0:T(1024)} %get-tuple-element.26) | copy-start | bytes 786436
  115.9 3.9 collective-permute-start.13
  117.3 5.4 collective-permute-start.14
  123.3 24.1 %collective-permute-start.15 = (f32[2,6,1,256]{3,2,1,0:T(1,128)S(1)}, f32[2,6,1,256]{3,2,1,0:T(1,128)S(1)}, u32[]{:S(2)}, u32[]{:S(2)}) collective-permute-start(f32[2,6,1,256]{3,2,1,0:T(1,128)S(1)} %get-tuple-element.43), channel_id=1, source_target_pairs={{0,1},{2,3},{4,5},{6,7},{8,9},{10,11},{12,13},{14,15},{16,17},{18,... | collective-permute-start | bytes 36872 | tf_op jit(solution)/shard_map/ppermute | solution.py:22
  125.3 22.1 %collective-permute-start.16 = (f32[2,6,1,256]{3,2,1,0:T(1,128)S(1)}, f32[2,6,1,256]{3,2,1,0:T(1,128)S(1)}, u32[]{:S(2)}, u32[]{:S(2)}) collective-permute-start(f32[2,6,1,256]{3,2,1,0:T(1,128)S(1)} %get-tuple-element.44), channel_id=1, source_target_pairs={{1,0},{3,2},{5,4},{7,6},{9,8},{11,10},{13,12},{15,14},{17,16},{19,... | collective-permute-start | bytes 36872 | tf_op jit(solution)/shard_map/ppermute | solution.py:23
  (21 other events, 35.4 us)
Sparse Core Ops, SparseCore 0:
  147.5 682.5 reduce-scatter.3
where the time goes:
time: 840 us; the launch traced here: 838 us
  waiting for transfers between devices  710 us (85%)
  local copies, waits for them, and re-layouts  49.4 us (6%)
  starting transfers between devices  39.9 us (5%)
  other arithmetic  21.1 us (3%)
  between operations  14.9 us (2%)
    unnamed x2, waiting for transfers between devices  678 us
    ppermute x8, starting transfers between devices, extended(): before = lax.ppermute(last, axis, up)  28.1 us
    unnamed x85, local copies, waits for them, and re-layouts  18.9 us
    ppermute x8, waiting for transfers between devices, extended(): after = lax.ppermute(leading, axis, down)  18.7 us
  transfers between devices with their start and end apart: 18, of which 9 were waited for; matrix products, arithmetic and copies ran while one was open for 6% of the time, Pallas kernels for 0%

commit v1 on v0

v1 whole, which is shorter than its diff:
```python
import functools

import jax
import jax.numpy as jnp
from jax import lax
from jax.experimental import pallas as pl
from jax.experimental.pallas import tpu as pltpu
from jax.sharding import PartitionSpec as P

MESH = pl.DeviceIdType.MESH
F32 = jnp.float32
BF16 = jnp.bfloat16
CX, CY, NZ = 4, 64, 256
PERFS = 256
NROCK = 8
RING = 64
RUN = 16
PAIRS = 8
LINKED = 1.5

LO, HI = 8, 8 + CY
BODY = pl.ds(LO, CY)

X_UP, X_DOWN = 0, 3
Y_START = 6
KH_OVER, KV_OVER = 7, 8
X2_UP, X2_DOWN, Y_SECOND = 9, 10, 11
FIELD_OVER = 12
AT_OVER = 16
K_UP, K_DOWN, K_Y = 17, 18, 19
S_UP, S_DOWN, S_Y = 20, 21, 22
P_UP, P_DOWN = 23, 24
R_FIRST = 25
R_SECOND = 41
N_SEM = 49
N_LOCAL = 16


def reciprocal(x):
    r = pl.reciprocal(x, approx=True)
    return r * (2.0 - x * r)


def harmonic(a, b):
    return (2.0 * a) * (b * reciprocal(a + b))


def split(x):
    high = x.astype(BF16)
    rest = x - high.astype(F32)
    mid = rest.astype(BF16)
    low = (rest - mid.astype(F32)).astype(BF16)
    return high, mid, low


def dot_nt(a, b):
    return lax.dot_general(a, b, (((1,), (1,)), ((), ())), preferred_element_type=F32)


def dot_nn(a, b):
    return lax.dot_general(a, b, (((1,), (0,)), ((), ())), preferred_element_type=F32)


def hot(index, rows):
    return lax.broadcasted_iota(jnp.int32, (rows, PERFS), 0) == index


def as_bf16(mask):
    return jnp.where(mask, 1.0, 0.0).astype(BF16)


def spread(row_hot, col_mask, value):
    total = None
    for piece in split(value):
        term = dot_nt(row_hot, jnp.where(col_mask, piece.astype(F32), 0.0).astype(BF16))
        total = term if total is None else total + term
    return total


def pick(field, row_mask, col_hot):
    total = None
    for piece in split(field):
        term = dot_nn(piece, col_hot)
        total = term if total is None else total + term
    return jnp.sum(jnp.where(row_mask, total, 0.0), axis=0, keepdims=True)


def body(
    unk, coe, rock, table, loc, pw, wi, pp, own, slo,
    out, rates,
    F0, F1, F2, T0, SH, KVC, WG, VM, RK, TX, TY, TZ, INV, BASE, WD, MOB,
    s_loc, s_pw, s_wi, s_pp, s_own, s_slo,
    ys0, yr0, ys1, yr1, ys2, yr2, ys3, yr3, ats, atr,
    part, got1, part2, got2, rate_buf,
    send, recv, lsem,
):
    sec, gx, gy = (lax.axis_index(a) for a in ("sec", "gx", "gy"))
    up = (sec, lax.rem(gx + 1, RING), gy)
    down = (sec, lax.rem(gx + RING - 1, RING), gy)
    side = (sec, gx, 1 - gy)
    other = (1 - sec, gx, gy)
    zc, y = lax.rem(gx, RUN), gx // RUN
    pair = y * 2 + gy
    first = [(sec, y * RUN + lax.rem(zc + d, RUN), gy) for d in range(1, RUN)]
    second = []
    for d in range(1, PAIRS):
        q = lax.rem(pair + d, PAIRS)
        second.append((sec, (q // 2) * RUN + zc, lax.rem(q, 2)))

    barrier = pltpu.get_barrier_semaphore()
    partners = [up, down, side, other] + first + second
    for dev in partners:
        pl.semaphore_signal(barrier, inc=1, device_id=dev, device_id_type=MESH)

    def local(i, src, dst):
        return pltpu.make_async_copy(src, dst, lsem.at[i])

    def remote(i, src, dst, dev):
        return pltpu.make_async_remote_copy(
            src_ref=src,
            dst_ref=dst,
            send_sem=send.at[i],
            recv_sem=recv.at[i],
            device_id=dev,
            device_id_type=MESH,
        )

    small = [
        local(0, loc, s_loc),
        local(1, pw, s_pw),
        local(2, wi, s_wi),
        local(3, pp, s_pp),
        local(4, own, s_own),
        local(5, slo, s_slo),
    ]
    for c in small:
        c.start()
    loads0 = [
        local(6, unk.at[0], F0.at[:, pl.ds(1, CX), BODY, :]),
        local(7, coe.at[0, 0], T0.at[0, pl.ds(1, CX), BODY, :]),
        local(8, coe.at[0, 3], T0.at[1, pl.ds(1, CX), BODY, :]),
        local(9, coe.at[0, pl.ds(1, 2)], KVC),
    ]
    loads1 = [local(6, unk.at[0], WG), local(7, coe.at[0], VM), local(8, rock, RK)]

    def wells():
        for c in small:
            c.wait()
        place = s_loc[...]
        row, col = lax.shift_right_logical(place, 8), jnp.bitwise_and(place, 255)
        row_mask, col_mask = hot(row, PERFS), hot(col, PERFS)
        row_hot, col_hot = as_bf16(row_mask), as_bf16(col_mask)
        live = s_pw[...] >= 0
        index = jnp.where(live, s_wi[...], 0.0)
        WD[0] = spread(row_hot, col_mask, index)
        WD[1] = spread(row_hot, col_mask, index * s_pp[...])
        well = jnp.maximum(s_pw[...], 0)
        w_row = hot(lax.shift_right_logical(well, 7), 64)
        w_col = as_bf16(hot(jnp.bitwise_and(well, 127), 128))

        def look(ref):
            found = dot_nn(ref[...].astype(F32).astype(BF16), w_col)
            return jnp.sum(jnp.where(w_row, found, 0.0), axis=0, keepdims=True).astype(jnp.int32)

        owner, slot = look(s_own), look(s_slo)
        o_gx, o_gy = lax.shift_right_logical(owner, 1), jnp.bitwise_and(owner, 1)
        order = (
            jnp.bitwise_and(o_gx, RUN - 1) * PAIRS + lax.shift_right_logical(o_gx, 4) * 2 + o_gy
        )
        return row_mask, col_hot, index, order, slot

    def rates_first(values, order, slot):
        own_mask, slot_hot = hot(order, RUN * PAIRS), as_bf16(hot(slot, 128))
        for a, value in enumerate(values):
            total = None
            for piece in split(value):
                lhs = jnp.where(own_mask, piece.astype(F32), 0.0).astype(BF16)
                term = dot_nt(lhs, slot_hot)
                total = term if total is None else total + term
            part[:, a] = total.reshape(RUN, PAIRS, 128)
        copies = [
            remote(R_FIRST + d, part.at[lax.rem(zc + d, RUN)], got1.at[d], first[d - 1])
            for d in far_first(RUN)
        ]
        for c in copies:
            c.start()
        return copies

    def rates_second(copies):
        for c in copies:
            c.wait()
        total = part[zc]
        for d in range(1, RUN):
            total = total + got1[d]
        part2[...] = jnp.zeros_like(part2)
        for a in range(2):
            for q in range(PAIRS):
                part2[q, a : a + 1] = total[a, q : q + 1]
        copies = [
            remote(R_SECOND + d, part2.at[lax.rem(pair + d, PAIRS)], got2.at[d], second[d - 1])
            for d in range(1, PAIRS)
        ]
        for c in copies:
            c.start()
        return copies

    def rates_last(copies):
        for c in copies:
            c.wait()
        total = part2[pair]
        for d in range(1, PAIRS):
            total = total + got2[d]
        rate_buf[...] = total[0:2]
        c = local(10, rate_buf, rates.at[0])
        c.start()
        return c

    def edge(ref, f, i):
        return jnp.where(gy == 0, ref[f, i, HI - 1 : HI, :], ref[f, i, LO : LO + 1, :])

    def set_edges(ref, f, i, row, zero):
        if zero:
            ref[f, i, HI : HI + 1, :] = jnp.where(gy == 0, row, 0.0)
            ref[f, i, LO - 1 : LO, :] = jnp.where(gy == 1, row, 0.0)
        else:
            ref[f, i, HI : HI + 1, :] = row
            ref[f, i, LO - 1 : LO, :] = row

    def x_face(f, a):
        face = harmonic(T0[f, a, BODY, :], T0[f, a + 1, BODY, :])
        if a == 0:
            face = jnp.where(gx == 0, 0.0, face)
        if a == CX:
            face = jnp.where(gx == RING - 1, 0.0, face)
        TX[f, a] = face

    def y_faces(f, i):
        TY[f, i - 1, LO : HI - 1] = harmonic(T0[f, i, LO : HI - 1, :], T0[f, i, LO + 1 : HI, :])

    def y_ends(f, i):
        for r in (LO - 1, HI - 1):
            TY[f, i - 1, r : r + 1] = harmonic(T0[f, i, r : r + 1, :], T0[f, i, r + 1 : r + 2, :])

    def z_faces(f, i, value):
        lane = lax.broadcasted_iota(jnp.int32, (CY, NZ), 1)
        face = harmonic(value, pltpu.roll(value, NZ - 1, 1))
        TZ[f, i - 1] = jnp.where(lane == NZ - 1, 0.0, face)

    def system(f, i, start):
        c = KVC[1, i - 1]
        tz = TZ[f, i - 1]
        total = (
            c + TX[f, i - 1] + TX[f, i] + TY[f, i - 1, LO - 1 : HI - 1] + TY[f, i - 1, LO:HI]
            + tz + pltpu.roll(tz, 1, 1)
        )
        base = c * start[f, i, BODY, :]
        if f == 0:
            rows = slice((i - 1) * CY, i * CY)
            total = total + WD[0, rows]
            base = base + WD[1, rows]
        INV[f, i - 1] = reciprocal(total)
        BASE[f, i - 1] = base

    def sweep(f, i, now, later):
        tz = TZ[f, i - 1]
        centre = now[f, i, BODY, :]
        total = (
            BASE[f, i - 1]
            + TX[f, i - 1] * now[f, i - 1, BODY, :]
            + TX[f, i] * now[f, i + 1, BODY, :]
            + TY[f, i - 1, LO - 1 : HI - 1] * now[f, i, LO - 1 : HI - 1, :]
            + TY[f, i - 1, LO:HI] * now[f, i, LO + 1 : HI + 1, :]
            + tz * pltpu.roll(centre, NZ - 1, 1)
            + pltpu.roll(tz * centre, 1, 1)
        )
        later[f, i, BODY, :] = total * INV[f, i - 1]

    def far_first(n):
        return sorted(range(1, n), key=lambda d: -min(d, n - d))

    def x_pair(i_up, i_down, ref, both=True, f=0):
        pick_ = (lambda a: ref.at[:, a, BODY, :]) if both else (lambda a: ref.at[f, a, BODY, :])
        return [
            remote(i_up, pick_(CX), pick_(0), up),
            remote(i_down, pick_(1), pick_(CX + 1), down),
        ]

    over = [
        remote(KH_OVER, coe.at[0, 0], T0.at[0, pl.ds(1, CX), BODY, :], other),
        remote(KV_OVER, coe.at[0, 1], KVC.at[0], other),
    ]
    fields_over = [
        remote(FIELD_OVER + i - 1, F2.at[:, i, BODY, :], F2.at[:, i, BODY, :], other)
        for i in range(1, CX + 1)
    ]
    at_over = remote(AT_OVER, ats, atr, other)
    layers = range(1, CX + 1)

    @pl.when(sec == 0)
    def _():
        for c in loads0:
            c.start()
        pl.semaphore_wait(barrier, len(partners))
        halo_x = []
        for s, dev, src, dst in ((X_UP, up, CX - 1, 0), (X_DOWN, down, 0, CX + 1)):
            halo_x += [
                remote(s, unk.at[0, :, src], F0.at[:, dst, BODY, :], dev),
                remote(s + 1, coe.at[0, 0, src], T0.at[0, dst, BODY, :], dev),
                remote(s + 2, coe.at[0, 3, src], T0.at[1, dst, BODY, :], dev),
            ]
        for c in halo_x:
            c.start()
        for c in loads0:
            c.wait()
        for f in range(2):
            for i in layers:
                r = f * CX + i - 1
                ys0[r : r + 1] = edge(F0, f, i)
                ys0[r + 8 : r + 9] = edge(T0, f, i)
        halo_y = remote(Y_START, ys0, yr0, side)
        halo_y.start()
        for c in over:
            c.start()
        for f in range(2):
            for i in layers:
                z_faces(f, i, KVC[0, i - 1] if f == 0 else T0[1, i, BODY, :])
                y_faces(f, i)
            for a in range(1, CX):
                x_face(f, a)
        row_mask, col_hot, index, order, slot = wells()
        halo_y.wait()
        for f in range(2):
            for i in layers:
                r = f * CX + i - 1
                set_edges(F0, f, i, yr0[r : r + 1], False)
                set_edges(T0, f, i, yr0[r + 8 : r + 9], True)
                y_ends(f, i)
            for i in (2, 3):
                system(f, i, F0)
                sweep(f, i, F0, F1)
        for c in halo_x:
            c.wait()
        for f in range(2):
            for a in (0, CX):
                x_face(f, a)
            for i in (1, CX):
                system(f, i, F0)
                sweep(f, i, F0, F1)
        halo_x = x_pair(X2_UP, X2_DOWN, F1)
        for c in halo_x:
            c.start()
        for f in range(2):
            for i in layers:
                r = f * CX + i - 1
                ys1[r : r + 1] = edge(F1, f, i)
        halo_y = remote(Y_SECOND, ys1, yr1, side)
        halo_y.start()
        halo_y.wait()
        for f in range(2):
            for i in layers:
                r = f * CX + i - 1
                set_edges(F1, f, i, yr1[r : r + 1], False)
        for i in (2, 3):
            for f in range(2):
                sweep(f, i, F1, F2)
            fields_over[i - 1].start()
        for c in halo_x:
            c.wait()
        for i in (1, CX):
            for f in range(2):
                sweep(f, i, F1, F2)
            fields_over[i - 1].start()
        save = local(11, F2.at[:, pl.ds(1, CX), BODY, :], out.at[0])
        save.start()
        pressure = pick(F2[0, 1 : CX + 1, BODY, :].reshape(CX * CY, NZ), row_mask, col_hot)
        warmth = pick(F2[1, 1 : CX + 1, BODY, :].reshape(CX * CY, NZ), row_mask, col_hot)
        ats[...] = jnp.zeros_like(ats)
        ats[0:1] = pressure
        ats[1:2] = warmth
        at_over.start()
        q = index * (s_pp[...] - pressure)
        copies = rates_first((q, q * warmth), order, slot)
        copies = rates_second(copies)
        last = rates_last(copies)
        for c in over + fields_over + [at_over]:
            c.wait_send()
        save.wait()
        last.wait()

    @pl.when(sec == 1)
    def _():
        for c in loads1:
            c.start()
        pl.semaphore_wait(barrier, len(partners))
        for c in loads1:
            c.wait()
        for i in range(CX):
            kind = RK[i]
            ends = []
            masks = [kind == t for t in range(1, NROCK)]
            for k in range(3):
                e = jnp.full((CY, NZ), table[0, k], F32)
                for t in range(1, NROCK):
                    e = jnp.where(masks[t - 1], table[t, k], e)
                ends.append(e)
            water, gas = WG[0, i], WG[1, i]
            oil = 1.0 - water - gas
            MOB[0, i] = ends[0] * water * water * reciprocal(VM[1, i])
            MOB[1, i] = ends[1] * oil * oil * reciprocal(VM[2, i])
            MOB[2, i] = ends[2] * gas * gas * reciprocal(VM[3, i])
        row_mask, col_hot, index, order, slot = wells()
        lw, lo, lg = (pick(MOB[k].reshape(CX * CY, NZ), row_mask, col_hot) for k in range(3))

        over[0].wait_recv()
        halo_k = x_pair(K_UP, K_DOWN, T0, False)
        for c in halo_k:
            c.start()
        ys2[...] = jnp.zeros_like(ys2)
        for i in layers:
            ys2[i - 1 : i] = edge(T0, 0, i)
        halo_ky = remote(K_Y, ys2, yr2, side)
        halo_ky.start()
        for i in layers:
            y_faces(0, i)
        for a in range(1, CX):
            x_face(0, a)
        over[1].wait_recv()
        for i in layers:
            z_faces(0, i, KVC[0, i - 1])
        for c in halo_k:
            c.wait()
        for a in (0, CX):
            x_face(0, a)
        halo_ky.wait()
        for i in layers:
            set_edges(T0, 0, i, yr2[i - 1 : i], True)
            y_ends(0, i)

        for i in (2, 3, 1, 4):
            fields_over[i - 1].wait_recv()
            other_mob = MOB[1, i - 1] * jnp.exp(LINKED * (F2[1, i, BODY, :] - 1.0))
            part_all = reciprocal(MOB[0, i - 1] + other_mob + MOB[2, i - 1])
            SH[0, i, BODY, :] = MOB[0, i - 1] * part_all
            SH[1, i, BODY, :] = MOB[2, i - 1] * part_all
        halo_s = x_pair(S_UP, S_DOWN, SH) + x_pair(P_UP, P_DOWN, F2, False)
        for c in halo_s:
            c.start()
        ys3[...] = jnp.zeros_like(ys3)
        for i in layers:
            ys3[i - 1 : i] = edge(F2, 0, i)
            ys3[i + 3 : i + 4] = edge(SH, 0, i)
            ys3[i + 7 : i + 8] = edge(SH, 1, i)
        halo_sy = remote(S_Y, ys3, yr3, side)
        halo_sy.start()

        at_over.wait_recv()
        q = index * (s_pp[...] - atr[0:1])
        lo = lo * jnp.exp(LINKED * (atr[1:2] - 1.0))
        scaled = q * reciprocal(lw + lo + lg)
        copies = rates_first((scaled * lw, scaled * lg), order, slot)

        halo_sy.wait()
        for i in layers:
            set_edges(F2, 0, i, yr3[i - 1 : i], False)
            set_edges(SH, 0, i, yr3[i + 3 : i + 4], False)
            set_edges(SH, 1, i, yr3[i + 7 : i + 8], False)
        for c in halo_s:
            c.wait()

        def through(flow, shares):
            pos, neg = jnp.maximum(flow, 0.0), jnp.minimum(flow, 0.0)
            return [pos * a + neg * b for a, b in shares]

        for i in layers:
            p = F2[0, i, BODY, :]
            s = [SH[a, i, BODY, :] for a in range(2)]
            tz = TZ[0, i - 1]
            west = through(
                TX[0, i - 1] * (F2[0, i - 1, BODY, :] - p),
                [(SH[a, i - 1, BODY, :], s[a]) for a in range(2)],
            )
            east = through(
                TX[0, i] * (p - F2[0, i + 1, BODY, :]),
                [(s[a], SH[a, i + 1, BODY, :]) for a in range(2)],
            )
            south = through(
                TY[0, i - 1, LO - 1 : HI - 1] * (F2[0, i, LO - 1 : HI - 1, :] - p),
                [(SH[a, i, LO - 1 : HI - 1, :], s[a]) for a in range(2)],
            )
            north = through(
                TY[0, i - 1, LO:HI] * (p - F2[0, i, LO + 1 : HI + 1, :]),
                [(s[a], SH[a, i, LO + 1 : HI + 1, :]) for a in range(2)],
            )
            top = through(
                tz * (p - pltpu.roll(p, NZ - 1, 1)),
                [(s[a], pltpu.roll(s[a], NZ - 1, 1)) for a in range(2)],
            )
            rows = slice((i - 1) * CY, i * CY)
            rate = WD[1, rows] - WD[0, rows] * p
            inverse = reciprocal(VM[0, i - 1])
            for a in range(2):
                net = west[a] - east[a] + south[a] - north[a] + pltpu.roll(top[a], 1, 1) - top[a]
                WG[a, i - 1] = WG[a, i - 1] + (net + rate * s[a]) * inverse
        save = local(11, WG, out.at[0])
        save.start()
        copies = rates_second(copies)
        last = rates_last(copies)
        save.wait()
        last.wait()


def per_device(unk, coe, rock, table, loc, pw, wi, pp, own, slo):
    any_ = pl.BlockSpec(memory_space=pl.ANY)
    row = lambda a: a.reshape(1, PERFS)
    vm = lambda *s: pltpu.VMEM(s, F32)
    halo = (2, CX + 2, CY + 16, NZ)
    return pl.pallas_call(
        body,
        out_shape=(
            jax.ShapeDtypeStruct((1, 2, CX, CY, NZ), F32),
            jax.ShapeDtypeStruct((1, 2, 128), F32),
        ),
        in_specs=[any_] * 3 + [pl.BlockSpec(memory_space=pltpu.SMEM)] + [any_] * 6,
        out_specs=(any_, any_),
        scratch_shapes=[
            vm(*halo), vm(*halo), vm(*halo), vm(*halo), vm(*halo),
            vm(2, CX, CY, NZ),
            vm(2, CX, CY, NZ),
            vm(4, CX, CY, NZ),
            pltpu.VMEM((CX, CY, NZ), jnp.int32),
            vm(2, CX + 1, CY, NZ), vm(2, CX, CY + 16, NZ), vm(2, CX, CY, NZ),
            vm(2, CX, CY, NZ), vm(2, CX, CY, NZ),
            vm(2, CX * CY, NZ),
            vm(3, CX, CY, NZ),
            pltpu.VMEM((1, PERFS), jnp.int32), pltpu.VMEM((1, PERFS), jnp.int32),
            vm(1, PERFS), vm(1, PERFS),
            pltpu.VMEM((64, 128), jnp.int32), pltpu.VMEM((64, 128), jnp.int32),
            vm(16, NZ), vm(16, NZ), vm(8, NZ), vm(8, NZ), vm(8, NZ), vm(8, NZ),
            vm(16, NZ), vm(16, NZ),
            vm(8, PERFS), vm(8, PERFS),
            vm(RUN, 2, PAIRS, 128), vm(RUN, 2, PAIRS, 128),
            vm(PAIRS, 8, 128), vm(PAIRS, 8, 128), vm(2, 128),
            pltpu.SemaphoreType.DMA((N_SEM,)),
            pltpu.SemaphoreType.DMA((N_SEM,)),
            pltpu.SemaphoreType.DMA((N_LOCAL,)),
        ],
        compiler_params=pltpu.CompilerParams(
            collective_id=0, has_side_effects=True, vmem_limit_bytes=40 * 2**20
        ),
    )(
        unk, coe, rock, table, row(loc), row(pw), row(wi), row(pp),
        own.reshape(64, 128), slo.reshape(64, 128),
    )


def solution(mesh):
    in_specs = (
        P("sec", None, "gx", "gy", None),
        P("sec", None, "gx", "gy", None),
        P("gx", "gy", None),
        P(),
        P(("gx", "gy")),
        P(("gx", "gy")),
        P(("gx", "gy")),
        P(("gx", "gy")),
        P(),
        P(),
    )
    out_specs = (P("sec", None, "gx", "gy", None), P("sec", None, ("gx", "gy")))
    return jax.shard_map(
        per_device, mesh=mesh, in_specs=in_specs, out_specs=out_specs, check_vma=False
    )
```

time: 840 us -> 57.9 us (0.07)
  the two profiles are of different devices: /device:TPU:2 before, /device:TPU:6 now
where the time goes in v1:
time: 57.9 us; the launch traced here: 57.5 us
  Pallas kernels  49.4 us (85%)
  local copies, waits for them, and re-layouts  7.48 us (13%)
  between operations  0.66 us (1%)
    pallas_call x1, Pallas kernels, per_device(): pl.pallas_call(body, out_shape=(jax.ShapeDtypeStruct((1, 2, CX, CY, NZ),...  49.4 us
    unnamed x23, local copies, waits for them, and re-layouts  7.48 us

profile of v1, /device:TPU:6, one launch (start us, length us, event | category | flops | bytes accessed | tf_op | source)
XLA Modules:
  0.0 57.5 jit_solution(4708187019868520288)
XLA Ops:
  0.6 0.0 copy-start.9
  0.6 0.7 %copy-done.9 = f32[8,3]{0,1:T(4,128)S(1)} copy-done((f32[8,3]{0,1:T(4,128)S(1)}, f32[8,3]{0,1:T(4,128)}, u32[]{:S(2)}) %copy-start.9) | copy-done | bytes 120
  1.3 0.0 copy-start.5
  1.3 0.0 copy-start.6
  1.3 0.0 copy-start.7
  1.3 0.0 copy-start.8
  1.3 0.1 copy.12.table
  1.4 0.6 %copy-done.5 = s32[256]{0:T(256)S(1)} copy-done((s32[256]{0:T(256)S(1)}, s32[256]{0:T(256)}, u32[]{:S(2)}) %copy-start.5) | copy-done | bytes 1048
  2.0 0.0 copy-done.6
  2.0 0.0 copy-done.7
  2.0 0.0 copy-done.8
  2.0 0.0 copy-start
  2.0 1.2 %copy-done = f32[1,4,4,64,256]{4,3,2,1,0:T(8,128)S(1)} copy-done((f32[1,4,4,64,256]{4,3,2,1,0:T(8,128)S(1)}, f32[1,4,4,64,256]{4,3,2,1,0:T(8,128)}, u32[]{:S(2)}) %copy-start) | copy-done | bytes 1048600
  3.3 0.0 copy-start.1
  3.3 1.0 %copy-done.1 = f32[1,2,4,64,256]{4,3,2,1,0:T(8,128)S(1)} copy-done((f32[1,2,4,64,256]{4,3,2,1,0:T(8,128)S(1)}, f32[1,2,4,64,256]{4,3,2,1,0:T(8,128)}, u32[]{:S(2)}) %copy-start.1) | copy-done | bytes 524312
  4.3 0.0 copy-start.2
  4.3 0.9 %copy-done.2 = s32[4,64,256]{2,1,0:T(8,128)S(1)} copy-done((s32[4,64,256]{2,1,0:T(8,128)S(1)}, s32[4,64,256]{2,1,0:T(8,128)}, u32[]{:S(2)}) %copy-start.2) | copy-done | bytes 262168
  5.3 0.0 copy-start.3
  5.3 0.8 %copy-done.3 = s32[8192]{0:T(1024)S(1)} copy-done((s32[8192]{0:T(1024)S(1)}, s32[8192]{0:T(1024)}, u32[]{:S(2)}) %copy-start.3) | copy-done | bytes 32792
  6.0 0.0 copy-start.4
  6.0 0.8 %copy-done.4 = s32[8192]{0:T(1024)S(1)} copy-done((s32[8192]{0:T(1024)S(1)}, s32[8192]{0:T(1024)}, u32[]{:S(2)}) %copy-start.4) | copy-done | bytes 32792
  6.8 49.4 %shard_map.113 = (f32[1,2,4,64,256]{4,3,2,1,0:T(8,128)S(1)}, f32[1,2,128]{2,1,0:T(2,128)S(1)}) custom-call(f32[1,2,4,64,256]{4,3,2,1,0:T(8,128)S(1)} %copy-done.1, f32[1,4,4,64,256]{4,3,2,1,0:T(8,128)S(1)} %copy-done, s32[4,64,256]{2,1,0:T(8,128)S(1)} %copy-done.2, f32[8,3]{1,0:T(8,128)S(1)} %copy.12.table, s32[1,256]{1,0:T(1,128)S(1)} %bitcast.8, ...), custom_call_target="tpu_custom_call" | custom-call | tf_op jit(solution)/shard_map/pallas_call | solution.py:517
  56.2 0.8 %copy.15 = f32[1,2,4,64,256]{4,3,2,1,0:T(8,128)} copy(f32[1,2,4,64,256]{4,3,2,1,0:T(8,128)S(1)} %get-tuple-element.4) | data formatting | bytes 1048576
  57.0 0.6 copy.16
Async XLA Ops:
  0.6 0.7 %copy-start.9 = (f32[8,3]{0,1:T(4,128)S(1)}, f32[8,3]{0,1:T(4,128)}, u32[]{:S(2)}) copy-start(f32[8,3]{0,1:T(4,128)} %param.13) | copy-start | bytes 292
  1.3 0.7 %copy-start.5 = (s32[256]{0:T(256)S(1)}, s32[256]{0:T(256)}, u32[]{:S(2)}) copy-start(s32[256]{0:T(256)} %param.14) | copy-start | bytes 3076
  1.3 0.7 %copy-start.6 = (s32[256]{0:T(256)S(1)}, s32[256]{0:T(256)}, u32[]{:S(2)}) copy-start(s32[256]{0:T(256)} %param.15) | copy-start | bytes 3076
  1.3 0.7 %copy-start.7 = (f32[256]{0:T(256)S(1)}, f32[256]{0:T(256)}, u32[]{:S(2)}) copy-start(f32[256]{0:T(256)} %param.16) | copy-start | bytes 3076
  1.3 0.7 %copy-start.8 = (f32[256]{0:T(256)S(1)}, f32[256]{0:T(256)}, u32[]{:S(2)}) copy-start(f32[256]{0:T(256)} %param.17) | copy-start | bytes 3076
  2.0 1.2 %copy-start = (f32[1,4,4,64,256]{4,3,2,1,0:T(8,128)S(1)}, f32[1,4,4,64,256]{4,3,2,1,0:T(8,128)}, u32[]{:S(2)}) copy-start(f32[1,4,4,64,256]{4,3,2,1,0:T(8,128)} %coe.1) | copy-start | bytes 3145732
  3.3 1.0 %copy-start.1 = (f32[1,2,4,64,256]{4,3,2,1,0:T(8,128)S(1)}, f32[1,2,4,64,256]{4,3,2,1,0:T(8,128)}, u32[]{:S(2)}) copy-start(f32[1,2,4,64,256]{4,3,2,1,0:T(8,128)} %unk.1) | copy-start | bytes 1572868
  4.3 0.9 %copy-start.2 = (s32[4,64,256]{2,1,0:T(8,128)S(1)}, s32[4,64,256]{2,1,0:T(8,128)}, u32[]{:S(2)}) copy-start(s32[4,64,256]{2,1,0:T(8,128)} %rock.1) | copy-start | bytes 786436
  5.3 0.8 %copy-start.3 = (s32[8192]{0:T(1024)S(1)}, s32[8192]{0:T(1024)}, u32[]{:S(2)}) copy-start(s32[8192]{0:T(1024)} %param.18) | copy-start | bytes 98308
  6.0 0.8 %copy-start.4 = (s32[8192]{0:T(1024)S(1)}, s32[8192]{0:T(1024)}, u32[]{:S(2)}) copy-start(s32[8192]{0:T(1024)} %param.19) | copy-start | bytes 98308

commit v2 on v1

--- a/solution.py
+++ b/solution.py
@@ -21,18 +21,21 @@
 LO, HI = 8, 8 + CY
 BODY = pl.ds(LO, CY)
 
-X_UP, X_DOWN = 0, 3
-Y_START = 6
-KH_OVER, KV_OVER = 7, 8
-X2_UP, X2_DOWN, Y_SECOND = 9, 10, 11
-FIELD_OVER = 12
-AT_OVER = 16
-K_UP, K_DOWN, K_Y = 17, 18, 19
-S_UP, S_DOWN, S_Y = 20, 21, 22
-P_UP, P_DOWN = 23, 24
-R_FIRST = 25
-R_SECOND = 41
-N_SEM = 49
+X_UP, X_DOWN = 0, 4
+Y_START = 8
+KH_OVER = 9
+KV_CROSS, KV_ON = 10, 12
+X2_UP, X2_DOWN = 14, 16
+Y_SECOND = 18
+MAIN_OVER = 19
+REST_OVER = 20
+AT_OVER = 26
+K_UP, K_DOWN, K_Y = 27, 28, 29
+S_UP, S_DOWN, S_Y = 30, 31, 32
+P_UP, P_DOWN, P_Y = 33, 34, 35
+R_FIRST = 36
+R_SECOND = 52
+N_SEM = 60
 N_LOCAL = 16
 
 
@@ -88,9 +91,9 @@
 def body(
     unk, coe, rock, table, loc, pw, wi, pp, own, slo,
     out, rates,
-    F0, F1, F2, T0, SH, KVC, WG, VM, RK, TX, TY, TZ, INV, BASE, WD, MOB,
+    F0, F1, F2, T0, SH, KVC, RL, WG, VM, RK, TX, TY, TZ, INV, BASE, WD, MOB,
     s_loc, s_pw, s_wi, s_pp, s_own, s_slo,
-    ys0, yr0, ys1, yr1, ys2, yr2, ys3, yr3, ats, atr,
+    ys0, yr0, ys1, yr1, ys2, yr2, ys3, yr3, ys4, yr4, ats, atr,
     part, got1, part2, got2, rate_buf,
     send, recv, lsem,
 ):
@@ -99,6 +102,7 @@
     down = (sec, lax.rem(gx + RING - 1, RING), gy)
     side = (sec, gx, 1 - gy)
     other = (1 - sec, gx, gy)
+    cross = (1 - sec, gx, 1 - gy)
     zc, y = lax.rem(gx, RUN), gx // RUN
     pair = y * 2 + gy
     first = [(sec, y * RUN + lax.rem(zc + d, RUN), gy) for d in range(1, RUN)]
@@ -108,7 +112,7 @@
         second.append((sec, (q // 2) * RUN + zc, lax.rem(q, 2)))
 
     barrier = pltpu.get_barrier_semaphore()
-    partners = [up, down, side, other] + first + second
+    partners = [up, down, side, other, cross] + first + second
     for dev in partners:
         pl.semaphore_signal(barrier, inc=1, device_id=dev, device_id_type=MESH)
 
@@ -285,14 +289,20 @@
             remote(i_down, pick_(1), pick_(CX + 1), down),
         ]
 
-    over = [
-        remote(KH_OVER, coe.at[0, 0], T0.at[0, pl.ds(1, CX), BODY, :], other),
-        remote(KV_OVER, coe.at[0, 1], KVC.at[0], other),
-    ]
-    fields_over = [
-        remote(FIELD_OVER + i - 1, F2.at[:, i, BODY, :], F2.at[:, i, BODY, :], other)
-        for i in range(1, CX + 1)
-    ]
+    kh_over = remote(KH_OVER, coe.at[0, 0], T0.at[0, pl.ds(1, CX), BODY, :], other)
+    halves = [pl.ds(0, 2), pl.ds(2, 2)]
+    kv_cross = [remote(KV_CROSS + c, coe.at[0, 1, h], RL.at[h], cross) for c, h in enumerate(halves)]
+    kv_on = [remote(KV_ON + c, RL.at[h], KVC.at[0, h], side) for c, h in enumerate(halves)]
+    main_rows = pl.ds(pl.multiple_of(LO + 8 * gy, 8), CY - 8)
+    edge_rows = pl.ds(pl.multiple_of(HI - 8 - (CY - 8) * gy, 8), 8)
+    inner = F2.at[:, pl.ds(2, 2), main_rows, :]
+    main_over = remote(MAIN_OVER, inner, inner, other)
+    rest_over = []
+    for f in range(2):
+        views = [F2.at[f, 1, BODY, :], F2.at[f, CX, BODY, :], F2.at[f, pl.ds(2, 2), edge_rows, :]]
+        rest_over.append(
+            [remote(REST_OVER + 3 * f + n, v, v, other) for n, v in enumerate(views)]
+        )
     at_over = remote(AT_OVER, ats, atr, other)
     layers = range(1, CX + 1)
 
@@ -302,14 +312,16 @@
             c.start()
         pl.semaphore_wait(barrier, len(partners))
         halo_x = []
-        for s, dev, src, dst in ((X_UP, up, CX - 1, 0), (X_DOWN, down, 0, CX + 1)):
-            halo_x += [
-                remote(s, unk.at[0, :, src], F0.at[:, dst, BODY, :], dev),
-                remote(s + 1, coe.at[0, 0, src], T0.at[0, dst, BODY, :], dev),
-                remote(s + 2, coe.at[0, 3, src], T0.at[1, dst, BODY, :], dev),
-            ]
-        for c in halo_x:
-            c.start()
+        for f in range(2):
+            group = []
+            for s, dev, src, dst in ((X_UP, up, CX - 1, 0), (X_DOWN, down, 0, CX + 1)):
+                group += [
+                    remote(s + 2 * f, unk.at[0, f, src], F0.at[f, dst, BODY, :], dev),
+                    remote(s + 2 * f + 1, coe.at[0, 3 * f, src], T0.at[f, dst, BODY, :], dev),
+                ]
+            for c in group:
+                c.start()
+            halo_x.append(group)
         for c in loads0:
             c.wait()
         for f in range(2):
@@ -319,7 +331,8 @@
                 ys0[r + 8 : r + 9] = edge(T0, f, i)
         halo_y = remote(Y_START, ys0, yr0, side)
         halo_y.start()
-        for c in over:
+        kh_over.start()
+        for c in kv_cross:
             c.start()
         for f in range(2):
             for i in layers:
@@ -338,51 +351,65 @@
             for i in (2, 3):
                 system(f, i, F0)
                 sweep(f, i, F0, F1)
-        for c in halo_x:
-            c.wait()
-        for f in range(2):
+                F1[f, i, HI : HI + 1, :] = jnp.zeros((1, NZ), F32)
+                F1[f, i, LO - 1 : LO, :] = jnp.zeros((1, NZ), F32)
+        halo_x2 = []
+        for f in range(2):
+            for c in halo_x[f]:
+                c.wait()
             for a in (0, CX):
                 x_face(f, a)
             for i in (1, CX):
                 system(f, i, F0)
                 sweep(f, i, F0, F1)
-        halo_x = x_pair(X2_UP, X2_DOWN, F1)
-        for c in halo_x:
-            c.start()
+            halo_x2.append(x_pair(X2_UP + f, X2_DOWN + f, F1, False, f))
+            for c in halo_x2[f]:
+                c.start()
         for f in range(2):
             for i in layers:
                 r = f * CX + i - 1
                 ys1[r : r + 1] = edge(F1, f, i)
         halo_y = remote(Y_SECOND, ys1, yr1, side)
         halo_y.start()
+        for f in range(2):
+            for i in (2, 3):
+                sweep(f, i, F1, F2)
+        main_over.start()
         halo_y.wait()
-        for f in range(2):
-            for i in layers:
-                r = f * CX + i - 1
-                set_edges(F1, f, i, yr1[r : r + 1], False)
-        for i in (2, 3):
-            for f in range(2):
+        for at, r, t in ((0, HI - 1, HI - 1), (1, LO, LO - 1)):
+
+            @pl.when(gy == at)
+            def _(r=r, t=t):
+                for f in range(2):
+                    for i in (2, 3):
+                        n = f * CX + i - 1
+                        more = TY[f, i - 1, t : t + 1] * INV[f, i - 1, r - LO : r - LO + 1]
+                        F2[f, i, r : r + 1, :] = F2[f, i, r : r + 1, :] + more * yr1[n : n + 1]
+
+        for f in range(2):
+            for i in (1, CX):
+                n = f * CX + i - 1
+                set_edges(F1, f, i, yr1[n : n + 1], False)
+            for c in halo_x2[f]:
+                c.wait()
+            for i in (1, CX):
                 sweep(f, i, F1, F2)
-            fields_over[i - 1].start()
-        for c in halo_x:
-            c.wait()
-        for i in (1, CX):
-            for f in range(2):
-                sweep(f, i, F1, F2)
-            fields_over[i - 1].start()
-        save = local(11, F2.at[:, pl.ds(1, CX), BODY, :], out.at[0])
-        save.start()
         pressure = pick(F2[0, 1 : CX + 1, BODY, :].reshape(CX * CY, NZ), row_mask, col_hot)
         warmth = pick(F2[1, 1 : CX + 1, BODY, :].reshape(CX * CY, NZ), row_mask, col_hot)
         ats[...] = jnp.zeros_like(ats)
         ats[0:1] = pressure
         ats[1:2] = warmth
         at_over.start()
+        for f in (1, 0):
+            for c in rest_over[f]:
+                c.start()
+        save = local(11, F2.at[:, pl.ds(1, CX), BODY, :], out.at[0])
+        save.start()
         q = index * (s_pp[...] - pressure)
         copies = rates_first((q, q * warmth), order, slot)
         copies = rates_second(copies)
         last = rates_last(copies)
-        for c in over + fields_over + [at_over]:
+        for c in [kh_over, main_over, at_over] + kv_cross + rest_over[0] + rest_over[1]:
             c.wait_send()
         save.wait()
         last.wait()
@@ -399,19 +426,23 @@
             ends = []
             masks = [kind == t for t in range(1, NROCK)]
             for k in range(3):
-                e = jnp.full((CY, NZ), table[0, k], F32)
+                e = jnp.full((CY, NZ), table[k, 0], F32)
                 for t in range(1, NROCK):
-                    e = jnp.where(masks[t - 1], table[t, k], e)
+                    e = jnp.where(masks[t - 1], table[k, t], e)
                 ends.append(e)
             water, gas = WG[0, i], WG[1, i]
             oil = 1.0 - water - gas
             MOB[0, i] = ends[0] * water * water * reciprocal(VM[1, i])
             MOB[1, i] = ends[1] * oil * oil * reciprocal(VM[2, i])
             MOB[2, i] = ends[2] * gas * gas * reciprocal(VM[3, i])
+        kv_cross[0].wait_recv()
+        kv_on[0].start()
         row_mask, col_hot, index, order, slot = wells()
         lw, lo, lg = (pick(MOB[k].reshape(CX * CY, NZ), row_mask, col_hot) for k in range(3))
-
-        over[0].wait_recv()
+        kv_cross[1].wait_recv()
+        kv_on[1].start()
+
+        kh_over.wait_recv()
         halo_k = x_pair(K_UP, K_DOWN, T0, False)
         for c in halo_k:
             c.start()
@@ -424,7 +455,8 @@
             y_faces(0, i)
         for a in range(1, CX):
             x_face(0, a)
-        over[1].wait_recv()
+        for c in kv_on:
+            c.wait()
         for i in layers:
             z_faces(0, i, KVC[0, i - 1])
         for c in halo_k:
@@ -436,35 +468,46 @@
             set_edges(T0, 0, i, yr2[i - 1 : i], True)
             y_ends(0, i)
 
-        for i in (2, 3, 1, 4):
-            fields_over[i - 1].wait_recv()
-            other_mob = MOB[1, i - 1] * jnp.exp(LINKED * (F2[1, i, BODY, :] - 1.0))
-            part_all = reciprocal(MOB[0, i - 1] + other_mob + MOB[2, i - 1])
-            SH[0, i, BODY, :] = MOB[0, i - 1] * part_all
-            SH[1, i, BODY, :] = MOB[2, i - 1] * part_all
-        halo_s = x_pair(S_UP, S_DOWN, SH) + x_pair(P_UP, P_DOWN, F2, False)
-        for c in halo_s:
-            c.start()
-        ys3[...] = jnp.zeros_like(ys3)
-        for i in layers:
-            ys3[i - 1 : i] = edge(F2, 0, i)
-            ys3[i + 3 : i + 4] = edge(SH, 0, i)
-            ys3[i + 7 : i + 8] = edge(SH, 1, i)
-        halo_sy = remote(S_Y, ys3, yr3, side)
-        halo_sy.start()
-
+        main_over.wait_recv()
         at_over.wait_recv()
         q = index * (s_pp[...] - atr[0:1])
         lo = lo * jnp.exp(LINKED * (atr[1:2] - 1.0))
         scaled = q * reciprocal(lw + lo + lg)
         copies = rates_first((scaled * lw, scaled * lg), order, slot)
+        for c in rest_over[1]:
+            c.wait_recv()
+        for i in (1, 4, 2, 3):
+            other_mob = MOB[1, i - 1] * jnp.exp(LINKED * (F2[1, i, BODY, :] - 1.0))
+            part_all = reciprocal(MOB[0, i - 1] + other_mob + MOB[2, i - 1])
+            SH[0, i, BODY, :] = MOB[0, i - 1] * part_all
+            SH[1, i, BODY, :] = MOB[2, i - 1] * part_all
+        halo_s = x_pair(S_UP, S_DOWN, SH)
+        for c in halo_s:
+            c.start()
+        for i in layers:
+            ys3[i - 1 : i] = edge(SH, 0, i)
+            ys3[i + 3 : i + 4] = edge(SH, 1, i)
+        halo_sy = remote(S_Y, ys3, yr3, side)
+        halo_sy.start()
+        for c in rest_over[0]:
+            c.wait_recv()
+        halo_p = x_pair(P_UP, P_DOWN, F2, False)
+        for c in halo_p:
+            c.start()
+        ys4[...] = jnp.zeros_like(ys4)
+        for i in layers:
+            ys4[i - 1 : i] = edge(F2, 0, i)
+        halo_py = remote(P_Y, ys4, yr4, side)
+        halo_py.start()
+        copies = rates_second(copies)
 
         halo_sy.wait()
-        for i in layers:
-            set_edges(F2, 0, i, yr3[i - 1 : i], False)
-            set_edges(SH, 0, i, yr3[i + 3 : i + 4], False)
-            set_edges(SH, 1, i, yr3[i + 7 : i + 8], False)
-        for c in halo_s:
+        halo_py.wait()
+        for i in layers:
+            set_edges(F2, 0, i, yr4[i - 1 : i], False)
+            set_edges(SH, 0, i, yr3[i - 1 : i], False)
+            set_edges(SH, 1, i, yr3[i + 3 : i + 4], False)
+        for c in halo_s + halo_p:
             c.wait()
 
         def through(flow, shares):
@@ -503,7 +546,6 @@
                 WG[a, i - 1] = WG[a, i - 1] + (net + rate * s[a]) * inverse
         save = local(11, WG, out.at[0])
         save.start()
-        copies = rates_second(copies)
         last = rates_last(copies)
         save.wait()
         last.wait()
@@ -524,7 +566,7 @@
         out_specs=(any_, any_),
         scratch_shapes=[
             vm(*halo), vm(*halo), vm(*halo), vm(*halo), vm(*halo),
-            vm(2, CX, CY, NZ),
+            vm(2, CX, CY, NZ), vm(CX, CY, NZ),
             vm(2, CX, CY, NZ),
             vm(4, CX, CY, NZ),
             pltpu.VMEM((CX, CY, NZ), jnp.int32),
@@ -536,7 +578,7 @@
             vm(1, PERFS), vm(1, PERFS),
             pltpu.VMEM((64, 128), jnp.int32), pltpu.VMEM((64, 128), jnp.int32),
             vm(16, NZ), vm(16, NZ), vm(8, NZ), vm(8, NZ), vm(8, NZ), vm(8, NZ),
-            vm(16, NZ), vm(16, NZ),
+            vm(8, NZ), vm(8, NZ), vm(8, NZ), vm(8, NZ),
             vm(8, PERFS), vm(8, PERFS),
             vm(RUN, 2, PAIRS, 128), vm(RUN, 2, PAIRS, 128),
             vm(PAIRS, 8, 128), vm(PAIRS, 8, 128), vm(2, 128),
@@ -545,10 +587,10 @@
             pltpu.SemaphoreType.DMA((N_LOCAL,)),
         ],
         compiler_params=pltpu.CompilerParams(
-            collective_id=0, has_side_effects=True, vmem_limit_bytes=40 * 2**20
+            collective_id=0, has_side_effects=True, vmem_limit_bytes=60 * 2**20
         ),
     )(
-        unk, coe, rock, table, row(loc), row(pw), row(wi), row(pp),
+        unk, coe, rock, table.T, row(loc), row(pw), row(wi), row(pp),
         own.reshape(64, 128), slo.reshape(64, 128),
     )
 

time: 57.9 us -> 43.4 us (0.75)
  the two profiles are of different devices: /device:TPU:6 before, /device:TPU:2 now
where the time goes in v2:
time: 43.4 us; the launch traced here: 43.2 us
  Pallas kernels  40.1 us (92%)
  local copies, waits for them, and re-layouts  2.44 us (6%)
  between operations  0.65 us (1%)
    pallas_call x1, Pallas kernels, per_device(): pl.pallas_call(body, out_shape=(jax.ShapeDtypeStruct((1, 2, CX, CY, NZ),...  40.1 us
    unnamed x4, local copies, waits for them, and re-layouts  2.44 us

profile of v2, /device:TPU:2, one launch (start us, length us, event | category | flops | bytes accessed | tf_op | source)
XLA Modules:
  0.0 43.2 jit_solution(2566101893406959559)
XLA Ops:
  0.6 40.1 %shard_map.113 = (f32[1,2,4,64,256]{4,3,2,1,0:T(8,128)}, f32[1,2,128]{2,1,0:T(2,128)}) custom-call(f32[1,2,4,64,256]{4,3,2,1,0:T(8,128)} %unk.1, f32[1,4,4,64,256]{4,3,2,1,0:T(8,128)} %coe.1, s32[4,64,256]{2,1,0:T(8,128)} %rock.1, f32[3,8]{1,0:T(4,128)} %bitcast.9, s32[1,256]{1,0:T(1,128)} %bitcast.10, s32[1,256]{1,0:T(1,128)} %bitcast.11, ...), custom_call_target="tpu_custom_call" | custom-call | tf_op jit(solution)/shard_map/pallas_call | solution.py:559
  40.8 0.0 copy-start
  40.8 1.9 %copy.14 = f32[1,2,4,64,256]{4,3,2,1,0:T(8,128)} copy(f32[1,2,4,64,256]{4,3,2,1,0:T(8,128)} %get-tuple-element.4) | data formatting | bytes 1048576
  42.7 0.0 copy-done
  42.7 0.6 %copy.15 = f32[1,2,128]{2,1,0:T(2,128)} copy(f32[1,2,128]{2,1,0:T(2,128)S(1)} %copy-done) | data formatting | bytes 2048
Async XLA Ops:
  40.8 1.9 %copy-start = (f32[1,2,128]{2,1,0:T(2,128)S(1)}, f32[1,2,128]{2,1,0:T(2,128)}, u32[]{:S(2)}) copy-start(f32[1,2,128]{2,1,0:T(2,128)} %get-tuple-element.5) | copy-start | bytes 3076

commit v3 on v2

--- a/solution.py
+++ b/solution.py
@@ -24,7 +24,7 @@
 X_UP, X_DOWN = 0, 4
 Y_START = 8
 KH_OVER = 9
-KV_CROSS, KV_ON = 10, 12
+KV_CROSS, KV_ON, KV_OVER = 10, 11, 12
 X2_UP, X2_DOWN = 14, 16
 Y_SECOND = 18
 MAIN_OVER = 19
@@ -290,9 +290,10 @@
         ]
 
     kh_over = remote(KH_OVER, coe.at[0, 0], T0.at[0, pl.ds(1, CX), BODY, :], other)
-    halves = [pl.ds(0, 2), pl.ds(2, 2)]
-    kv_cross = [remote(KV_CROSS + c, coe.at[0, 1, h], RL.at[h], cross) for c, h in enumerate(halves)]
-    kv_on = [remote(KV_ON + c, RL.at[h], KVC.at[0, h], side) for c, h in enumerate(halves)]
+    halves = [pl.ds(0, 3), pl.ds(3, 1)]
+    kv_cross = remote(KV_CROSS, coe.at[0, 1, halves[0]], RL, cross)
+    kv_on = remote(KV_ON, RL, KVC.at[0, halves[0]], side)
+    kv_over = remote(KV_OVER, coe.at[0, 1, halves[1]], KVC.at[0, halves[1]], other)
     main_rows = pl.ds(pl.multiple_of(LO + 8 * gy, 8), CY - 8)
     edge_rows = pl.ds(pl.multiple_of(HI - 8 - (CY - 8) * gy, 8), 8)
     inner = F2.at[:, pl.ds(2, 2), main_rows, :]
@@ -332,8 +333,7 @@
         halo_y = remote(Y_START, ys0, yr0, side)
         halo_y.start()
         kh_over.start()
-        for c in kv_cross:
-            c.start()
+        kv_cross.start()
         for f in range(2):
             for i in layers:
                 z_faces(f, i, KVC[0, i - 1] if f == 0 else T0[1, i, BODY, :])
@@ -403,13 +403,14 @@
         for f in (1, 0):
             for c in rest_over[f]:
                 c.start()
+        kv_over.start()
         save = local(11, F2.at[:, pl.ds(1, CX), BODY, :], out.at[0])
         save.start()
         q = index * (s_pp[...] - pressure)
         copies = rates_first((q, q * warmth), order, slot)
         copies = rates_second(copies)
         last = rates_last(copies)
-        for c in [kh_over, main_over, at_over] + kv_cross + rest_over[0] + rest_over[1]:
+        for c in [kh_over, kv_cross, kv_over, main_over, at_over] + rest_over[0] + rest_over[1]:
             c.wait_send()
         save.wait()
         last.wait()
@@ -435,12 +436,10 @@
             MOB[0, i] = ends[0] * water * water * reciprocal(VM[1, i])
             MOB[1, i] = ends[1] * oil * oil * reciprocal(VM[2, i])
             MOB[2, i] = ends[2] * gas * gas * reciprocal(VM[3, i])
-        kv_cross[0].wait_recv()
-        kv_on[0].start()
+        kv_cross.wait_recv()
+        kv_on.start()
         row_mask, col_hot, index, order, slot = wells()
         lw, lo, lg = (pick(MOB[k].reshape(CX * CY, NZ), row_mask, col_hot) for k in range(3))
-        kv_cross[1].wait_recv()
-        kv_on[1].start()
 
         kh_over.wait_recv()
         halo_k = x_pair(K_UP, K_DOWN, T0, False)
@@ -455,10 +454,6 @@
             y_faces(0, i)
         for a in range(1, CX):
             x_face(0, a)
-        for c in kv_on:
-            c.wait()
-        for i in layers:
-            z_faces(0, i, KVC[0, i - 1])
         for c in halo_k:
             c.wait()
         for a in (0, CX):
@@ -509,6 +504,10 @@
             set_edges(SH, 1, i, yr3[i + 3 : i + 4], False)
         for c in halo_s + halo_p:
             c.wait()
+        kv_on.wait()
+        kv_over.wait_recv()
+        for i in layers:
+            z_faces(0, i, KVC[0, i - 1])
 
         def through(flow, shares):
             pos, neg = jnp.maximum(flow, 0.0), jnp.minimum(flow, 0.0)
@@ -551,12 +550,28 @@
         last.wait()
 
 
+def hand_over(unknowns, sums, out, rates, held, held_sums, take, give):
+    parts = [(sums.at[0], held_sums, rates.at[0], 2 * CX)]
+    for f in range(2):
+        for i in range(CX):
+            parts.append((unknowns.at[0, f, i], held.at[f, i], out.at[0, f, i], f * CX + i))
+    inward = [pltpu.make_async_copy(a, b, take.at[n]) for a, b, _, n in parts]
+    outward = [pltpu.make_async_copy(b, c, give.at[n]) for _, b, c, n in parts]
+    for c in inward:
+        c.start()
+    for a, b in zip(inward, outward):
+        a.wait()
+        b.start()
+    for c in outward:
+        c.wait()
+
+
 def per_device(unk, coe, rock, table, loc, pw, wi, pp, own, slo):
     any_ = pl.BlockSpec(memory_space=pl.ANY)
     row = lambda a: a.reshape(1, PERFS)
     vm = lambda *s: pltpu.VMEM(s, F32)
     halo = (2, CX + 2, CY + 16, NZ)
-    return pl.pallas_call(
+    unknowns, sums = pl.pallas_call(
         body,
         out_shape=(
             jax.ShapeDtypeStruct((1, 2, CX, CY, NZ), F32),
@@ -566,7 +581,7 @@
         out_specs=(any_, any_),
         scratch_shapes=[
             vm(*halo), vm(*halo), vm(*halo), vm(*halo), vm(*halo),
-            vm(2, CX, CY, NZ), vm(CX, CY, NZ),
+            vm(2, CX, CY, NZ), vm(3, CY, NZ),
             vm(2, CX, CY, NZ),
             vm(4, CX, CY, NZ),
             pltpu.VMEM((CX, CY, NZ), jnp.int32),
@@ -593,6 +608,22 @@
         unk, coe, rock, table.T, row(loc), row(pw), row(wi), row(pp),
         own.reshape(64, 128), slo.reshape(64, 128),
     )
+    return pl.pallas_call(
+        hand_over,
+        out_shape=(
+            jax.ShapeDtypeStruct(unknowns.shape, F32),
+            jax.ShapeDtypeStruct(sums.shape, F32),
+        ),
+        in_specs=[any_, any_],
+        out_specs=(any_, any_),
+        scratch_shapes=[
+            vm(2, CX, CY, NZ),
+            vm(2, 128),
+            pltpu.SemaphoreType.DMA((2 * CX + 1,)),
+            pltpu.SemaphoreType.DMA((2 * CX + 1,)),
+        ],
+        compiler_params=pltpu.CompilerParams(vmem_limit_bytes=60 * 2**20),
+    )(unknowns, sums)
 
 
 def solution(mesh):

time: 43.4 us -> 39.8 us (0.917)
  local copies, waits for them, and re-layouts: 2.44 us -> 0 us
  Pallas kernels: 40.1 us -> 38.8 us
    pallas_call x1, Pallas kernels: 40.1 us -> 37 us  [per_device(): pl.pallas_call(body, out_shape=(jax.ShapeDtypeStruct((1, 2, CX, CY, NZ),...]
    unnamed x4 -> x0, local copies, waits for them, and re-layouts: 2.44 us -> none
    pallas_call x0 -> x1, Pallas kernels: none -> 1.85 us  [per_device(): pl.pallas_call(hand_over, out_shape=(jax.ShapeDtypeStruct(unknowns.shape,...]
where the time goes in v3:
time: 39.8 us; the launch traced here: 39.5 us
  Pallas kernels  38.8 us (97%)
  between operations  0.64 us (2%)
    pallas_call x1, Pallas kernels, per_device(): pl.pallas_call(body, out_shape=(jax.ShapeDtypeStruct((1, 2, CX, CY, NZ),...  37 us
    pallas_call x1, Pallas kernels, per_device(): pl.pallas_call(hand_over, out_shape=(jax.ShapeDtypeStruct(unknowns.shape,...  1.85 us

profile of v3, /device:TPU:2, one launch (start us, length us, event | category | flops | bytes accessed | tf_op | source)
XLA Modules:
  0.0 39.5 jit_solution(10171299270352775450)
XLA Ops:
  0.6 37.0 %shard_map.113 = (f32[1,2,4,64,256]{4,3,2,1,0:T(8,128)}, f32[1,2,128]{2,1,0:T(2,128)}) custom-call(f32[1,2,4,64,256]{4,3,2,1,0:T(8,128)} %unk.1, f32[1,4,4,64,256]{4,3,2,1,0:T(8,128)} %coe.1, s32[4,64,256]{2,1,0:T(8,128)} %rock.1, f32[3,8]{1,0:T(4,128)} %bitcast.9, s32[1,256]{1,0:T(1,128)} %bitcast.10, s32[1,256]{1,0:T(1,128)} %bitcast.11, ...), custom_call_target="tpu_custom_call" | custom-call | tf_op jit(solution)/shard_map/pallas_call | solution.py:574
  37.6 1.9 %shard_map.114 = (f32[1,2,4,64,256]{4,3,2,1,0:T(8,128)}, f32[1,2,128]{2,1,0:T(2,128)}) custom-call(f32[1,2,4,64,256]{4,3,2,1,0:T(8,128)} %get-tuple-element.4.unknowns, f32[1,2,128]{2,1,0:T(2,128)} %get-tuple-element.5.sums), custom_call_target="tpu_custom_call" | custom-call | tf_op jit(solution)/shard_map/pallas_call | solution.py:611

commit v4 on v3

--- a/solution.py
+++ b/solution.py
@@ -23,11 +23,10 @@
 
 X_UP, X_DOWN = 0, 4
 Y_START = 8
-KH_OVER = 9
+KH_OVER = 60
 KV_CROSS, KV_ON, KV_OVER = 10, 11, 12
 X2_UP, X2_DOWN = 14, 16
 Y_SECOND = 18
-MAIN_OVER = 19
 REST_OVER = 20
 AT_OVER = 26
 K_UP, K_DOWN, K_Y = 27, 28, 29
@@ -35,7 +34,8 @@
 P_UP, P_DOWN, P_Y = 33, 34, 35
 R_FIRST = 36
 R_SECOND = 52
-N_SEM = 60
+MAIN_OVER = 65
+N_SEM = 67
 N_LOCAL = 16
 
 
@@ -104,6 +104,12 @@
     other = (1 - sec, gx, gy)
     cross = (1 - sec, gx, 1 - gy)
     zc, y = lax.rem(gx, RUN), gx // RUN
+    core = lax.rem(gx, 2)
+    mate = (sec, gx + 1 - 2 * core, gy)
+    far = (sec, lax.rem(gx + RING - 1 + 2 * core, RING), gy)
+    near_far, near_mate = 1 + (CX - 1) * core, CX - (CX - 1) * core
+    halo_far, halo_mate = (CX + 1) * core, (CX + 1) * (1 - core)
+    others = 2 - core
     pair = y * 2 + gy
     first = [(sec, y * RUN + lax.rem(zc + d, RUN), gy) for d in range(1, RUN)]
     second = []
@@ -231,12 +237,11 @@
             ref[f, i, LO - 1 : LO, :] = row
 
     def x_face(f, a):
+        outside = jnp.logical_or(
+            jnp.logical_and(gx == 0, a == 0), jnp.logical_and(gx == RING - 1, a == CX)
+        )
         face = harmonic(T0[f, a, BODY, :], T0[f, a + 1, BODY, :])
-        if a == 0:
-            face = jnp.where(gx == 0, 0.0, face)
-        if a == CX:
-            face = jnp.where(gx == RING - 1, 0.0, face)
-        TX[f, a] = face
+        TX[f, a] = jnp.where(outside, 0.0, face)
 
     def y_faces(f, i):
         TY[f, i - 1, LO : HI - 1] = harmonic(T0[f, i, LO : HI - 1, :], T0[f, i, LO + 1 : HI, :])
@@ -259,7 +264,7 @@
         )
         base = c * start[f, i, BODY, :]
         if f == 0:
-            rows = slice((i - 1) * CY, i * CY)
+            rows = pl.ds((i - 1) * CY if isinstance(i, int) else pl.multiple_of((i - 1) * CY, CY), CY)
             total = total + WD[0, rows]
             base = base + WD[1, rows]
         INV[f, i - 1] = reciprocal(total)
@@ -289,18 +294,22 @@
             remote(i_down, pick_(1), pick_(CX + 1), down),
         ]
 
-    kh_over = remote(KH_OVER, coe.at[0, 0], T0.at[0, pl.ds(1, CX), BODY, :], other)
+    kh_over = [
+        remote(KH_OVER + i, coe.at[0, 0, i - 1], T0.at[0, i, BODY, :], other) for i in (1, CX, 2)
+    ]
+    kh_last = remote(KH_OVER + 3, coe.at[0, 0, 2], T0.at[0, 3, BODY, :], other)
+    kh_edges = remote(K_Y, yr0.at[pl.ds(8, 8)], yr2, other)
     halves = [pl.ds(0, 3), pl.ds(3, 1)]
     kv_cross = remote(KV_CROSS, coe.at[0, 1, halves[0]], RL, cross)
     kv_on = remote(KV_ON, RL, KVC.at[0, halves[0]], side)
     kv_over = remote(KV_OVER, coe.at[0, 1, halves[1]], KVC.at[0, halves[1]], other)
     main_rows = pl.ds(pl.multiple_of(LO + 8 * gy, 8), CY - 8)
     edge_rows = pl.ds(pl.multiple_of(HI - 8 - (CY - 8) * gy, 8), 8)
-    inner = F2.at[:, pl.ds(2, 2), main_rows, :]
-    main_over = remote(MAIN_OVER, inner, inner, other)
+    inner = [F2.at[f, pl.ds(others, 3), main_rows, :] for f in range(2)]
+    main_over = [remote(MAIN_OVER + f, v, v, other) for f, v in enumerate(inner)]
     rest_over = []
     for f in range(2):
-        views = [F2.at[f, 1, BODY, :], F2.at[f, CX, BODY, :], F2.at[f, pl.ds(2, 2), edge_rows, :]]
+        views = [F2.at[f, near_far, BODY, :], F2.at[f, pl.ds(others, 3), edge_rows, :]]
         rest_over.append(
             [remote(REST_OVER + 3 * f + n, v, v, other) for n, v in enumerate(views)]
         )
@@ -311,18 +320,6 @@
     def _():
         for c in loads0:
             c.start()
-        pl.semaphore_wait(barrier, len(partners))
-        halo_x = []
-        for f in range(2):
-            group = []
-            for s, dev, src, dst in ((X_UP, up, CX - 1, 0), (X_DOWN, down, 0, CX + 1)):
-                group += [
-                    remote(s + 2 * f, unk.at[0, f, src], F0.at[f, dst, BODY, :], dev),
-                    remote(s + 2 * f + 1, coe.at[0, 3 * f, src], T0.at[f, dst, BODY, :], dev),
-                ]
-            for c in group:
-                c.start()
-            halo_x.append(group)
         for c in loads0:
             c.wait()
         for f in range(2):
@@ -330,9 +327,24 @@
                 r = f * CX + i - 1
                 ys0[r : r + 1] = edge(F0, f, i)
                 ys0[r + 8 : r + 9] = edge(T0, f, i)
+        pl.semaphore_wait(barrier, len(partners))
         halo_y = remote(Y_START, ys0, yr0, side)
         halo_y.start()
-        kh_over.start()
+        halo_far_x, halo_mate_x = [], []
+        for f in range(2):
+            for s, dev, src, dst, group in (
+                (X_UP, far, near_far, halo_mate, halo_far_x),
+                (X_DOWN, mate, near_mate, halo_far, halo_mate_x),
+            ):
+                pair_ = [
+                    remote(s + 2 * f, unk.at[0, f, src - 1], F0.at[f, dst, BODY, :], dev),
+                    remote(s + 2 * f + 1, coe.at[0, 3 * f, src - 1], T0.at[f, dst, BODY, :], dev),
+                ]
+                for c in pair_:
+                    c.start()
+                group.append(pair_)
+        for c in kh_over:
+            c.start()
         kv_cross.start()
         for f in range(2):
             for i in layers:
@@ -342,67 +354,77 @@
                 x_face(f, a)
         row_mask, col_hot, index, order, slot = wells()
         halo_y.wait()
+        kh_edges.start()
         for f in range(2):
             for i in layers:
                 r = f * CX + i - 1
                 set_edges(F0, f, i, yr0[r : r + 1], False)
                 set_edges(T0, f, i, yr0[r + 8 : r + 9], True)
                 y_ends(f, i)
+                F1[f, i, HI : HI + 1, :] = jnp.zeros((1, NZ), F32)
+                F1[f, i, LO - 1 : LO, :] = jnp.zeros((1, NZ), F32)
             for i in (2, 3):
                 system(f, i, F0)
                 sweep(f, i, F0, F1)
-                F1[f, i, HI : HI + 1, :] = jnp.zeros((1, NZ), F32)
-                F1[f, i, LO - 1 : LO, :] = jnp.zeros((1, NZ), F32)
-        halo_x2 = []
         for f in range(2):
-            for c in halo_x[f]:
+            for c in halo_mate_x[f]:
                 c.wait()
-            for a in (0, CX):
-                x_face(f, a)
-            for i in (1, CX):
-                system(f, i, F0)
-                sweep(f, i, F0, F1)
-            halo_x2.append(x_pair(X2_UP + f, X2_DOWN + f, F1, False, f))
-            for c in halo_x2[f]:
-                c.start()
+            x_face(f, CX * (1 - core))
+            system(f, near_mate, F0)
+            sweep(f, near_mate, F0, F1)
+        mate_x2 = remote(X2_DOWN, F1.at[:, near_mate, BODY, :], F1.at[:, halo_far, BODY, :], mate)
+        mate_x2.start()
+        far_x2 = []
+        for f in (1, 0):
+            for c in halo_far_x[f]:
+                c.wait()
+            x_face(f, CX * core)
+            system(f, near_far, F0)
+            sweep(f, near_far, F0, F1)
+            c = remote(
+                X2_UP + f, F1.at[f, near_far, BODY, :], F1.at[f, halo_mate, BODY, :], far
+            )
+            c.start()
+            far_x2.append(c)
         for f in range(2):
             for i in layers:
                 r = f * CX + i - 1
                 ys1[r : r + 1] = edge(F1, f, i)
         halo_y = remote(Y_SECOND, ys1, yr1, side)
         halo_y.start()
-        for f in range(2):
-            for i in (2, 3):
-                sweep(f, i, F1, F2)
-        main_over.start()
+        mate_x2.wait()
+        for f in (1, 0):
+            for k in range(3):
+                sweep(f, others + k, F1, F2)
+            if f == 1:
+                main_over[1].start()
+                kh_last.start()
         halo_y.wait()
         for at, r, t in ((0, HI - 1, HI - 1), (1, LO, LO - 1)):
 
             @pl.when(gy == at)
             def _(r=r, t=t):
                 for f in range(2):
-                    for i in (2, 3):
+                    for k in range(3):
+                        i = others + k
                         n = f * CX + i - 1
                         more = TY[f, i - 1, t : t + 1] * INV[f, i - 1, r - LO : r - LO + 1]
-                        F2[f, i, r : r + 1, :] = F2[f, i, r : r + 1, :] + more * yr1[n : n + 1]
-
-        for f in range(2):
-            for i in (1, CX):
-                n = f * CX + i - 1
-                set_edges(F1, f, i, yr1[n : n + 1], False)
-            for c in halo_x2[f]:
-                c.wait()
-            for i in (1, CX):
-                sweep(f, i, F1, F2)
+                        row = yr1[pl.ds(n, 1)]
+                        F2[f, i, r : r + 1, :] = F2[f, i, r : r + 1, :] + more * row
+
+        for f, c in zip((1, 0), far_x2):
+            set_edges(F1, f, near_far, yr1[pl.ds(f * CX + near_far - 1, 1)], False)
+            c.wait()
+            sweep(f, near_far, F1, F2)
         pressure = pick(F2[0, 1 : CX + 1, BODY, :].reshape(CX * CY, NZ), row_mask, col_hot)
         warmth = pick(F2[1, 1 : CX + 1, BODY, :].reshape(CX * CY, NZ), row_mask, col_hot)
         ats[...] = jnp.zeros_like(ats)
         ats[0:1] = pressure
         ats[1:2] = warmth
         at_over.start()
-        for f in (1, 0):
-            for c in rest_over[f]:
-                c.start()
+        for c in rest_over[1] + rest_over[0]:
+            c.start()
+        main_over[0].start()
         kv_over.start()
         save = local(11, F2.at[:, pl.ds(1, CX), BODY, :], out.at[0])
         save.start()
@@ -410,7 +432,7 @@
         copies = rates_first((q, q * warmth), order, slot)
         copies = rates_second(copies)
         last = rates_last(copies)
-        for c in [kh_over, kv_cross, kv_over, main_over, at_over] + rest_over[0] + rest_over[1]:
+        for c in kh_over + main_over + [kh_last, kh_edges, kv_cross, kv_over, at_over] + rest_over[0] + rest_over[1]:
             c.wait_send()
         save.wait()
         last.wait()
@@ -441,35 +463,35 @@
         row_mask, col_hot, index, order, slot = wells()
         lw, lo, lg = (pick(MOB[k].reshape(CX * CY, NZ), row_mask, col_hot) for k in range(3))
 
-        kh_over.wait_recv()
+        for c in kh_over:
+            c.wait_recv()
         halo_k = x_pair(K_UP, K_DOWN, T0, False)
         for c in halo_k:
             c.start()
-        ys2[...] = jnp.zeros_like(ys2)
+        for i in (1, CX, 2):
+            y_faces(0, i)
+        x_face(0, 1)
+        kh_edges.wait_recv()
         for i in layers:
-            ys2[i - 1 : i] = edge(T0, 0, i)
-        halo_ky = remote(K_Y, ys2, yr2, side)
-        halo_ky.start()
-        for i in layers:
-            y_faces(0, i)
-        for a in range(1, CX):
+            set_edges(T0, 0, i, yr2[i - 1 : i], True)
+        for i in (1, CX, 2):
+            y_ends(0, i)
+        kh_last.wait_recv()
+        for a in (2, 3):
             x_face(0, a)
+        y_faces(0, 3)
+        y_ends(0, 3)
         for c in halo_k:
             c.wait()
         for a in (0, CX):
             x_face(0, a)
-        halo_ky.wait()
-        for i in layers:
-            set_edges(T0, 0, i, yr2[i - 1 : i], True)
-            y_ends(0, i)
-
-        main_over.wait_recv()
+
         at_over.wait_recv()
         q = index * (s_pp[...] - atr[0:1])
         lo = lo * jnp.exp(LINKED * (atr[1:2] - 1.0))
         scaled = q * reciprocal(lw + lo + lg)
         copies = rates_first((scaled * lw, scaled * lg), order, slot)
-        for c in rest_over[1]:
+        for c in rest_over[1] + main_over[1:]:
             c.wait_recv()
         for i in (1, 4, 2, 3):
             other_mob = MOB[1, i - 1] * jnp.exp(LINKED * (F2[1, i, BODY, :] - 1.0))
@@ -486,12 +508,18 @@
         halo_sy.start()
         for c in rest_over[0]:
             c.wait_recv()
-        halo_p = x_pair(P_UP, P_DOWN, F2, False)
-        for c in halo_p:
-            c.start()
+        far_p = remote(
+            P_UP, F2.at[0, near_far, BODY, :], F2.at[0, halo_mate, BODY, :], far
+        )
+        far_p.start()
         ys4[...] = jnp.zeros_like(ys4)
-        for i in layers:
-            ys4[i - 1 : i] = edge(F2, 0, i)
+        for at, r in ((0, HI - 1), (1, LO)):
+
+            @pl.when(gy == at)
+            def _(r=r):
+                for i in layers:
+                    ys4[i - 1 : i] = F2[0, i, r : r + 1, :]
+
         halo_py = remote(P_Y, ys4, yr4, side)
         halo_py.start()
         copies = rates_second(copies)
@@ -502,12 +530,18 @@
             set_edges(F2, 0, i, yr4[i - 1 : i], False)
             set_edges(SH, 0, i, yr3[i - 1 : i], False)
             set_edges(SH, 1, i, yr3[i + 3 : i + 4], False)
-        for c in halo_s + halo_p:
+        main_over[0].wait_recv()
+        mate_p = remote(
+            P_DOWN, F2.at[0, near_mate, BODY, :], F2.at[0, halo_far, BODY, :], mate
+        )
+        mate_p.start()
+        for c in halo_s + [far_p]:
             c.wait()
         kv_on.wait()
         kv_over.wait_recv()
         for i in layers:
             z_faces(0, i, KVC[0, i - 1])
+        mate_p.wait()
 
         def through(flow, shares):
             pos, neg = jnp.maximum(flow, 0.0), jnp.minimum(flow, 0.0)

time: 39.8 us -> 39 us (0.980)
  Pallas kernels: 38.8 us -> 37.7 us
    pallas_call x1, Pallas kernels: 37 us -> 35.8 us  [per_device(): pl.pallas_call(body, out_shape=(jax.ShapeDtypeStruct((1, 2, CX, CY, NZ),...]
where the time goes in v4:
time: 39 us; the launch traced here: 38.3 us
  Pallas kernels  37.7 us (97%)
  between operations  0.64 us (2%)
    pallas_call x1, Pallas kernels, per_device(): pl.pallas_call(body, out_shape=(jax.ShapeDtypeStruct((1, 2, CX, CY, NZ),...  35.8 us
    pallas_call x1, Pallas kernels, per_device(): pl.pallas_call(hand_over, out_shape=(jax.ShapeDtypeStruct(unknowns.shape,...  1.85 us

profile of v4, /device:TPU:2, one launch (start us, length us, event | category | flops | bytes accessed | tf_op | source)
XLA Modules:
  0.0 38.3 jit_solution(5364626571068944162)
XLA Ops:
  0.6 35.8 %shard_map.113 = (f32[1,2,4,64,256]{4,3,2,1,0:T(8,128)}, f32[1,2,128]{2,1,0:T(2,128)}) custom-call(f32[1,2,4,64,256]{4,3,2,1,0:T(8,128)} %unk.1, f32[1,4,4,64,256]{4,3,2,1,0:T(8,128)} %coe.1, s32[4,64,256]{2,1,0:T(8,128)} %rock.1, f32[3,8]{1,0:T(4,128)} %bitcast.9, s32[1,256]{1,0:T(1,128)} %bitcast.10, s32[1,256]{1,0:T(1,128)} %bitcast.11, ...), custom_call_target="tpu_custom_call" | custom-call | tf_op jit(solution)/shard_map/pallas_call | solution.py:608
  36.5 1.9 %shard_map.114 = (f32[1,2,4,64,256]{4,3,2,1,0:T(8,128)}, f32[1,2,128]{2,1,0:T(2,128)}) custom-call(f32[1,2,4,64,256]{4,3,2,1,0:T(8,128)} %get-tuple-element.4.unknowns, f32[1,2,128]{2,1,0:T(2,128)} %get-tuple-element.5.sums), custom_call_target="tpu_custom_call" | custom-call | tf_op jit(solution)/shard_map/pallas_call | solution.py:645

commit v5 on v4

--- a/solution.py
+++ b/solution.py
@@ -80,12 +80,13 @@
     return total
 
 
-def pick(field, row_mask, col_hot):
-    total = None
-    for piece in split(field):
-        term = dot_nn(piece, col_hot)
-        total = term if total is None else total + term
-    return jnp.sum(jnp.where(row_mask, total, 0.0), axis=0, keepdims=True)
+def pick(fields, row_mask, col_hot):
+    found = dot_nn(jnp.concatenate([p for field in fields for p in split(field)], axis=0), col_hot)
+    rows = []
+    for k in range(len(fields)):
+        a, b, c = (found[(3 * k + n) * PERFS : (3 * k + n + 1) * PERFS] for n in range(3))
+        rows.append(jnp.sum(jnp.where(row_mask, a + b + c, 0.0), axis=0, keepdims=True))
+    return rows
 
 
 def body(
@@ -181,13 +182,16 @@
 
     def rates_first(values, order, slot):
         own_mask, slot_hot = hot(order, RUN * PAIRS), as_bf16(hot(slot, 128))
-        for a, value in enumerate(values):
-            total = None
-            for piece in split(value):
-                lhs = jnp.where(own_mask, piece.astype(F32), 0.0).astype(BF16)
-                term = dot_nt(lhs, slot_hot)
-                total = term if total is None else total + term
-            part[:, a] = total.reshape(RUN, PAIRS, 128)
+        lhs = [
+            jnp.where(own_mask, piece.astype(F32), 0.0).astype(BF16)
+            for value in values
+            for piece in split(value)
+        ]
+        found = dot_nt(jnp.concatenate(lhs, axis=0), slot_hot)
+        size = RUN * PAIRS
+        for a in range(2):
+            u, v, w = (found[(3 * a + n) * size : (3 * a + n + 1) * size] for n in range(3))
+            part[:, a] = (u + v + w).reshape(RUN, PAIRS, 128)
         copies = [
             remote(R_FIRST + d, part.at[lax.rem(zc + d, RUN)], got1.at[d], first[d - 1])
             for d in far_first(RUN)
@@ -299,10 +303,10 @@
     ]
     kh_last = remote(KH_OVER + 3, coe.at[0, 0, 2], T0.at[0, 3, BODY, :], other)
     kh_edges = remote(K_Y, yr0.at[pl.ds(8, 8)], yr2, other)
-    halves = [pl.ds(0, 3), pl.ds(3, 1)]
-    kv_cross = remote(KV_CROSS, coe.at[0, 1, halves[0]], RL, cross)
-    kv_on = remote(KV_ON, RL, KVC.at[0, halves[0]], side)
-    kv_over = remote(KV_OVER, coe.at[0, 1, halves[1]], KVC.at[0, halves[1]], other)
+    three = pl.ds(core, 3)
+    kv_cross = remote(KV_CROSS, coe.at[0, 1, three], RL, cross)
+    kv_on = remote(KV_ON, RL, KVC.at[0, three], side)
+    kv_over = remote(KV_OVER, coe.at[0, 1, near_mate - 1], KVC.at[0, near_mate - 1], other)
     main_rows = pl.ds(pl.multiple_of(LO + 8 * gy, 8), CY - 8)
     edge_rows = pl.ds(pl.multiple_of(HI - 8 - (CY - 8) * gy, 8), 8)
     inner = [F2.at[f, pl.ds(others, 3), main_rows, :] for f in range(2)]
@@ -416,8 +420,8 @@
             set_edges(F1, f, near_far, yr1[pl.ds(f * CX + near_far - 1, 1)], False)
             c.wait()
             sweep(f, near_far, F1, F2)
-        pressure = pick(F2[0, 1 : CX + 1, BODY, :].reshape(CX * CY, NZ), row_mask, col_hot)
-        warmth = pick(F2[1, 1 : CX + 1, BODY, :].reshape(CX * CY, NZ), row_mask, col_hot)
+        finals = [F2[f, 1 : CX + 1, BODY, :].reshape(CX * CY, NZ) for f in range(2)]
+        pressure, warmth = pick(finals, row_mask, col_hot)
         ats[...] = jnp.zeros_like(ats)
         ats[0:1] = pressure
         ats[1:2] = warmth
@@ -425,12 +429,12 @@
         for c in rest_over[1] + rest_over[0]:
             c.start()
         main_over[0].start()
-        kv_over.start()
         save = local(11, F2.at[:, pl.ds(1, CX), BODY, :], out.at[0])
         save.start()
         q = index * (s_pp[...] - pressure)
         copies = rates_first((q, q * warmth), order, slot)
         copies = rates_second(copies)
+        kv_over.start()
         last = rates_last(copies)
         for c in kh_over + main_over + [kh_last, kh_edges, kv_cross, kv_over, at_over] + rest_over[0] + rest_over[1]:
             c.wait_send()
@@ -461,7 +465,7 @@
         kv_cross.wait_recv()
         kv_on.start()
         row_mask, col_hot, index, order, slot = wells()
-        lw, lo, lg = (pick(MOB[k].reshape(CX * CY, NZ), row_mask, col_hot) for k in range(3))
+        lw, lo, lg = pick([MOB[k].reshape(CX * CY, NZ) for k in range(3)], row_mask, col_hot)
 
         for c in kh_over:
             c.wait_recv()
@@ -530,6 +534,9 @@
             set_edges(F2, 0, i, yr4[i - 1 : i], False)
             set_edges(SH, 0, i, yr3[i - 1 : i], False)
             set_edges(SH, 1, i, yr3[i + 3 : i + 4], False)
+        kv_on.wait()
+        for k in range(3):
+            z_faces(0, core + k + 1, KVC[0, core + k])
         main_over[0].wait_recv()
         mate_p = remote(
             P_DOWN, F2.at[0, near_mate, BODY, :], F2.at[0, halo_far, BODY, :], mate
@@ -537,17 +544,18 @@
         mate_p.start()
         for c in halo_s + [far_p]:
             c.wait()
-        kv_on.wait()
-        kv_over.wait_recv()
-        for i in layers:
-            z_faces(0, i, KVC[0, i - 1])
-        mate_p.wait()
 
         def through(flow, shares):
             pos, neg = jnp.maximum(flow, 0.0), jnp.minimum(flow, 0.0)
             return [pos * a + neg * b for a, b in shares]
 
-        for i in layers:
+        saves = []
+        for k in range(CX):
+            i = near_far + k * (1 - 2 * core)
+            if k == CX - 1:
+                kv_over.wait_recv()
+                z_faces(0, i, KVC[0, i - 1])
+                mate_p.wait()
             p = F2[0, i, BODY, :]
             s = [SH[a, i, BODY, :] for a in range(2)]
             tz = TZ[0, i - 1]
@@ -571,17 +579,17 @@
                 tz * (p - pltpu.roll(p, NZ - 1, 1)),
                 [(s[a], pltpu.roll(s[a], NZ - 1, 1)) for a in range(2)],
             )
-            rows = slice((i - 1) * CY, i * CY)
+            rows = pl.ds(pl.multiple_of((i - 1) * CY, CY), CY)
             rate = WD[1, rows] - WD[0, rows] * p
             inverse = reciprocal(VM[0, i - 1])
             for a in range(2):
                 net = west[a] - east[a] + south[a] - north[a] + pltpu.roll(top[a], 1, 1) - top[a]
                 WG[a, i - 1] = WG[a, i - 1] + (net + rate * s[a]) * inverse
-        save = local(11, WG, out.at[0])
-        save.start()
+            saves.append(local(11 + k, WG.at[:, i - 1], out.at[0, :, i - 1]))
+            saves[-1].start()
         last = rates_last(copies)
-        save.wait()
-        last.wait()
+        for c in saves + [last]:
+            c.wait()
 
 
 def hand_over(unknowns, sums, out, rates, held, held_sums, take, give):

time: 39 us -> 38.5 us (0.987); the launches traced: 38.3 us -> 38.3 us
  no operation moved by 1% of the time
where the time goes in v5:
time: 38.5 us; the launch traced here: 38.3 us
  Pallas kernels  37.7 us (98%)
  between operations  0.64 us (2%)
    pallas_call x1, Pallas kernels, per_device(): pl.pallas_call(body, out_shape=(jax.ShapeDtypeStruct((1, 2, CX, CY, NZ),...  35.8 us
    pallas_call x1, Pallas kernels, per_device(): pl.pallas_call(hand_over, out_shape=(jax.ShapeDtypeStruct(unknowns.shape,...  1.85 us

profile of v5, /device:TPU:2, one launch (start us, length us, event | category | flops | bytes accessed | tf_op | source)
XLA Modules:
  0.0 38.3 jit_solution(17898999030830863936)
XLA Ops:
  0.6 35.8 %shard_map.113 = (f32[1,2,4,64,256]{4,3,2,1,0:T(8,128)}, f32[1,2,128]{2,1,0:T(2,128)}) custom-call(f32[1,2,4,64,256]{4,3,2,1,0:T(8,128)} %unk.1, f32[1,4,4,64,256]{4,3,2,1,0:T(8,128)} %coe.1, s32[4,64,256]{2,1,0:T(8,128)} %rock.1, f32[3,8]{1,0:T(4,128)} %bitcast.9, s32[1,256]{1,0:T(1,128)} %bitcast.10, s32[1,256]{1,0:T(1,128)} %bitcast.11, ...), custom_call_target="tpu_custom_call" | custom-call | tf_op jit(solution)/shard_map/pallas_call | solution.py:616
  36.5 1.9 %shard_map.114 = (f32[1,2,4,64,256]{4,3,2,1,0:T(8,128)}, f32[1,2,128]{2,1,0:T(2,128)}) custom-call(f32[1,2,4,64,256]{4,3,2,1,0:T(8,128)} %get-tuple-element.4.unknowns, f32[1,2,128]{2,1,0:T(2,128)} %get-tuple-element.5.sums), custom_call_target="tpu_custom_call" | custom-call | tf_op jit(solution)/shard_map/pallas_call | solution.py:653

commit v6 on v5

--- a/solution.py
+++ b/solution.py
@@ -595,8 +595,7 @@
 def hand_over(unknowns, sums, out, rates, held, held_sums, take, give):
     parts = [(sums.at[0], held_sums, rates.at[0], 2 * CX)]
     for f in range(2):
-        for i in range(CX):
-            parts.append((unknowns.at[0, f, i], held.at[f, i], out.at[0, f, i], f * CX + i))
+        parts.append((unknowns.at[0, f], held.at[f], out.at[0, f], f))
     inward = [pltpu.make_async_copy(a, b, take.at[n]) for a, b, _, n in parts]
     outward = [pltpu.make_async_copy(b, c, give.at[n]) for _, b, c, n in parts]
     for c in inward:

time: 38.5 us -> 38.5 us (level)
  no operation moved by 1% of the time
where the time goes in v6:
time: 38.5 us; the launch traced here: 38.4 us
  Pallas kernels  37.7 us (98%)
  between operations  0.64 us (2%)
    pallas_call x1, Pallas kernels, per_device(): pl.pallas_call(body, out_shape=(jax.ShapeDtypeStruct((1, 2, CX, CY, NZ),...  35.8 us
    pallas_call x1, Pallas kernels, per_device(): pl.pallas_call(hand_over, out_shape=(jax.ShapeDtypeStruct(unknowns.shape,...  1.9 us

profile of v6, /device:TPU:2, one launch (start us, length us, event | category | flops | bytes accessed | tf_op | source)
XLA Modules:
  0.0 38.4 jit_solution(6628280879675656005)
XLA Ops:
  0.6 35.8 %shard_map.113 = (f32[1,2,4,64,256]{4,3,2,1,0:T(8,128)}, f32[1,2,128]{2,1,0:T(2,128)}) custom-call(f32[1,2,4,64,256]{4,3,2,1,0:T(8,128)} %unk.1, f32[1,4,4,64,256]{4,3,2,1,0:T(8,128)} %coe.1, s32[4,64,256]{2,1,0:T(8,128)} %rock.1, f32[3,8]{1,0:T(4,128)} %bitcast.9, s32[1,256]{1,0:T(1,128)} %bitcast.10, s32[1,256]{1,0:T(1,128)} %bitcast.11, ...), custom_call_target="tpu_custom_call" | custom-call | tf_op jit(solution)/shard_map/pallas_call | solution.py:615
  36.5 1.9 %shard_map.114 = (f32[1,2,4,64,256]{4,3,2,1,0:T(8,128)}, f32[1,2,128]{2,1,0:T(2,128)}) custom-call(f32[1,2,4,64,256]{4,3,2,1,0:T(8,128)} %get-tuple-element.4.unknowns, f32[1,2,128]{2,1,0:T(2,128)} %get-tuple-element.5.sums), custom_call_target="tpu_custom_call" | custom-call | tf_op jit(solution)/shard_map/pallas_call | solution.py:652

commit v7 on v6

--- a/solution.py
+++ b/solution.py
@@ -335,11 +335,11 @@
         halo_y = remote(Y_START, ys0, yr0, side)
         halo_y.start()
         halo_far_x, halo_mate_x = [], []
-        for f in range(2):
-            for s, dev, src, dst, group in (
-                (X_UP, far, near_far, halo_mate, halo_far_x),
-                (X_DOWN, mate, near_mate, halo_far, halo_mate_x),
-            ):
+        for s, dev, src, dst, group in (
+            (X_UP, far, near_far, halo_mate, halo_far_x),
+            (X_DOWN, mate, near_mate, halo_far, halo_mate_x),
+        ):
+            for f in range(2):
                 pair_ = [
                     remote(s + 2 * f, unk.at[0, f, src - 1], F0.at[f, dst, BODY, :], dev),
                     remote(s + 2 * f + 1, coe.at[0, 3 * f, src - 1], T0.at[f, dst, BODY, :], dev),
@@ -379,7 +379,7 @@
         mate_x2 = remote(X2_DOWN, F1.at[:, near_mate, BODY, :], F1.at[:, halo_far, BODY, :], mate)
         mate_x2.start()
         far_x2 = []
-        for f in (1, 0):
+        for f in (0, 1):
             for c in halo_far_x[f]:
                 c.wait()
             x_face(f, CX * core)
@@ -416,7 +416,7 @@
                         row = yr1[pl.ds(n, 1)]
                         F2[f, i, r : r + 1, :] = F2[f, i, r : r + 1, :] + more * row
 
-        for f, c in zip((1, 0), far_x2):
+        for f, c in zip((0, 1), far_x2):
             set_edges(F1, f, near_far, yr1[pl.ds(f * CX + near_far - 1, 1)], False)
             c.wait()
             sweep(f, near_far, F1, F2)

time: 38.5 us -> 38.5 us (level)
  no operation moved by 1% of the time
where the time goes in v7:
time: 38.5 us; the launch traced here: 38.4 us
  Pallas kernels  37.7 us (98%)
  between operations  0.64 us (2%)
    pallas_call x1, Pallas kernels, per_device(): pl.pallas_call(body, out_shape=(jax.ShapeDtypeStruct((1, 2, CX, CY, NZ),...  35.8 us
    pallas_call x1, Pallas kernels, per_device(): pl.pallas_call(hand_over, out_shape=(jax.ShapeDtypeStruct(unknowns.shape,...  1.9 us

profile of v7, /device:TPU:2, one launch (start us, length us, event | category | flops | bytes accessed | tf_op | source)
XLA Modules:
  0.0 38.4 jit_solution(8625155508439890904)
XLA Ops:
  0.6 35.8 %shard_map.113 = (f32[1,2,4,64,256]{4,3,2,1,0:T(8,128)}, f32[1,2,128]{2,1,0:T(2,128)}) custom-call(f32[1,2,4,64,256]{4,3,2,1,0:T(8,128)} %unk.1, f32[1,4,4,64,256]{4,3,2,1,0:T(8,128)} %coe.1, s32[4,64,256]{2,1,0:T(8,128)} %rock.1, f32[3,8]{1,0:T(4,128)} %bitcast.9, s32[1,256]{1,0:T(1,128)} %bitcast.10, s32[1,256]{1,0:T(1,128)} %bitcast.11, ...), custom_call_target="tpu_custom_call" | custom-call | tf_op jit(solution)/shard_map/pallas_call | solution.py:615
  36.5 1.9 %shard_map.114 = (f32[1,2,4,64,256]{4,3,2,1,0:T(8,128)}, f32[1,2,128]{2,1,0:T(2,128)}) custom-call(f32[1,2,4,64,256]{4,3,2,1,0:T(8,128)} %get-tuple-element.4.unknowns, f32[1,2,128]{2,1,0:T(2,128)} %get-tuple-element.5.sums), custom_call_target="tpu_custom_call" | custom-call | tf_op jit(solution)/shard_map/pallas_call | solution.py:652
